TPU v7x, 256 devices: a whole 4x4x8 slice. The times are simulated.
256 devices in a mesh: dp: 16 (over x, z_lo, core), tensor: 16 (over y, z_hi).
Axes of the slice: x: 4, y: 4, z: 8 (z_hi: 4, z_lo: 2; z = z_hi * 2 + z_lo), core: 2. Of those that a mesh axis runs over, the one named last changes fastest.
Arguments:
- gate_pre: bfloat16 [2048, 28672], P('dp', 'tensor'), may hold values from -6 to 6
- up_pre: bfloat16 [2048, 28672], P('dp', 'tensor'), may hold values from -6 to 6
- down_rotated: bfloat16 [28672, 8192], P('tensor', 'dp'), may hold values from -0.03125 to 0.03125
- exponents: int32 [224, 8192], P('tensor', 'dp'), may hold values from -10 to -7
- signs: int32 [28672], P('tensor'), may hold values from 0 to 1
- out_grad: bfloat16 [2048, 8192], P('tensor', 'dp'), may hold values from -6 to 6
Outputs:
- layer_out: bfloat16 [2048, 8192], P('tensor', 'dp')
- grad_down: float32 [28672, 8192], P('tensor', 'dp')
- grad_gate: bfloat16 [2048, 28672], P('dp', 'tensor')
- grad_up: bfloat16 [2048, 28672], P('dp', 'tensor')
All inputs are finite; a program needn't handle non-finite values.
Results may differ from a plain program's by a relative error of at most 0.025.
Values may be sent and summed in bfloat16 or wider, within the bound.
A program may use at most 128 MiB of HBM per device.

v0:
```python
import jax
import jax.numpy as jnp
import numpy as np
from jax import lax
from jax.sharding import PartitionSpec as P

WALSH = 128
GROUP = 128


HIGH = lax.Precision.HIGHEST


def partner_2(array, axis, distance):
    return lax.ppermute(array, axis, [(i, i ^ 1 << distance) for i in range(lax.axis_size(axis))])


def sylvester(order):
    left = np.arange(order)[:, None]
    right = np.arange(order)[None, :]
    anded = left & right
    parity = np.zeros((order, order), np.int64)
    for bit in range(max(order.bit_length(), 1)):
        parity = parity + (anded >> bit & 1)
    table = 1.0 - 2.0 * (parity % 2)
    return jnp.asarray(table / np.sqrt(order), jnp.float32)


def cosine(order):
    rows = np.arange(order)[:, None]
    cols = np.arange(order)[None, :]
    table = np.sqrt(2.0 / order) * np.cos(np.pi * (2 * rows + 1) * cols / (2.0 * order))
    table = np.where(cols == 0, np.sqrt(1.0 / order), table)
    return jnp.asarray(table, jnp.float32)


def cross_shard(values):
    count = lax.axis_size("tensor")
    index = lax.axis_index("tensor")
    for bit in range(count.bit_length() - 1):
        partner = partner_2(values.astype(jnp.bfloat16), "tensor", bit).astype(values.dtype)
        upper = index >> bit & 1 == 1
        values = jnp.where(upper, partner - values, values + partner)
    return values * (1.0 / np.sqrt(count))


def on_device(gate_pre, up_pre, down_rotated, exponents, signs, out_grad):
    rows, width = gate_pre.shape
    cos_len = width // WALSH
    walsh = sylvester(WALSH)
    cos_table = cosine(cos_len)
    gate = gate_pre.astype(jnp.float32)
    up = up_pre.astype(jnp.float32)
    active = jax.nn.silu(gate)
    hidden = (active * up).astype(jnp.bfloat16)
    sign_f = (2 * signs - 1).astype(jnp.float32)
    shaped = (hidden.astype(jnp.float32) * sign_f).reshape(rows, cos_len, WALSH)
    shaped = jnp.einsum("amk,kl->aml", shaped, walsh, precision=HIGH)
    shaped = jnp.einsum("amk,mn->ank", shaped, cos_table, precision=HIGH)
    rotated = cross_shard(shaped.reshape(rows, width)).astype(jnp.bfloat16)
    groups, columns = exponents.shape
    scale = jnp.broadcast_to(
        jnp.exp2(exponents.astype(jnp.float32))[:, None, :], (groups, GROUP, columns)
    ).reshape(groups * GROUP, columns)
    squash = jnp.tanh(down_rotated.astype(jnp.float32) / (7.0 * scale))
    weight_q = (7.0 * scale * squash).astype(jnp.bfloat16)
    all_rows = lax.all_gather(rotated, "dp", axis=0, tiled=True)
    piece = lax.slice_in_dim(all_rows, 0, out_grad.shape[0] * lax.axis_size("tensor"), axis=0)
    layer_out = lax.psum_scatter(
        jnp.dot(piece, weight_q, preferred_element_type=jnp.float32).astype(jnp.bfloat16),
        "tensor",
        scatter_dimension=0,
        tiled=True,
    )
    grad_all = lax.all_gather(out_grad, "tensor", axis=0, tiled=True)
    grad_w = lax.dot_general(
        all_rows, grad_all, (((0,), (0,)), ((), ())), preferred_element_type=jnp.float32
    )
    grad_down = grad_w * (1.0 - squash * squash)
    piece = grad_all
    grad_rot = lax.psum_scatter(
        lax.dot_general(
            piece, weight_q, (((1,), (1,)), ((), ())), preferred_element_type=jnp.float32
        ).astype(jnp.bfloat16),
        "dp",
        scatter_dimension=0,
        tiled=True,
    ).astype(jnp.float32)
    mixed = cross_shard(grad_rot).reshape(rows, cos_len, WALSH)
    mixed = jnp.einsum("ank,mn->amk", mixed, cos_table, precision=HIGH)
    mixed = jnp.einsum("amk,kl->aml", mixed, walsh, precision=HIGH)
    grad_hidden = mixed.reshape(rows, width) * sign_f
    sigma = jax.nn.sigmoid(gate)
    grad_gate = (grad_hidden * up * sigma * (1.0 + gate * (1.0 - sigma))).astype(jnp.bfloat16)
    grad_up = (grad_hidden * active).astype(jnp.bfloat16)
    return (layer_out, grad_down, grad_gate, grad_up)


def solution(mesh):
    return jax.shard_map(
        on_device,
        mesh=mesh,
        in_specs=(
            P("dp", "tensor"),
            P("dp", "tensor"),
            P("tensor", "dp"),
            P("tensor", "dp"),
            P("tensor"),
            P("tensor", "dp"),
        ),
        out_specs=(P("tensor", "dp"), P("tensor", "dp"), P("dp", "tensor"), P("dp", "tensor")),
        check_vma=False,
    )
```

profile of v0, /device:TPU:2, one launch (start us, length us, event | category | flops | bytes accessed | tf_op | source)
XLA Modules:
  0.0 500.4 jit_solution(8255427140927207355)
XLA Ops:
  7.2 0.0 all-gather.5.cloned.1.call-start
  7.2 0.7 all-gather.5.cloned.1.call-update
  7.9 0.0 reduce-scatter.7.cloned.1.call-start
  7.9 0.8 exponential_multiply_fusion
  8.7 4.2 fusion.1
  12.9 59.7 %all-gather.5.cloned.1.call-done = bf16[2048,512]{1,0:T(8,128)(2,1)} async-done(((bf16[128,512]{1,0:T(8,128)(2,1)}), bf16[2048,512]{1,0:T(8,128)(2,1)}) %all-gather.5.cloned.1.call-update) | async-done | bytes 2097168 | tf_op jit(solution)/shard_map/all_gather | solution.py:75
  72.6 7.7 %fusion = bf16[2048,1792]{0,1:T(8,128)(2,1)} fusion(bf16[1792,512]{1,0:T(8,128)(2,1)S(1)} %get-tuple-element.15, bf16[2048,512]{1,0:T(8,128)(2,1)} %all-gather.5.cloned.1.call-done), kind=kOutput, calls=%fused_computation.1 | convolution fusion | flops 3761766400 | bytes 11272192 | tf_op jit(solution)/shard_map/dot_general | solution.py:82
  80.3 0.0 copy-done
  80.3 10.0 %copy.37 = bf16[2048,1792]{1,0:T(8,128)(2,1)} copy(bf16[2048,1792]{0,1:T(8,128)(2,1)} %fusion) | data formatting | bytes 14680064
  90.3 0.0 reduce-scatter.7.cloned.1.call-update
  90.4 0.0 copy-start.4
  90.4 0.0 copy-start.5
  90.4 0.0 all-gather.3.cloned.1.call-start
  90.4 86.0 %reduce-scatter.7.cloned.1.call-done = bf16[128,1792]{1,0:T(8,128)(2,1)} async-done(((bf16[2048,1792]{1,0:T(8,128)(2,1)}), bf16[128,1792]{1,0:T(8,128)(2,1)}) %reduce-scatter.7.cloned.1.call-update) | async-done | bytes 458768
  176.4 1.3 copy.38
  177.7 2.6 collective-permute-start.4
  180.3 20.7 %collective-permute-done.4 = bf16[128,1792]{0,1:T(8,128)(2,1)S(1)} collective-permute-done((bf16[128,1792]{0,1:T(8,128)(2,1)S(1)}, bf16[128,1792]{0,1:T(8,128)(2,1)S(1)}, u32[]{:S(2)}, u32[]{:S(2)}) %collective-permute-start.4) | collective-permute-done | bytes 458784 | tf_op jit(solution)/shard_map/ppermute | solution.py:15
  201.0 0.2 fusion.25
  201.2 5.0 %collective-permute-start.5 = (bf16[128,1792]{0,1:T(8,128)(2,1)S(1)}, bf16[128,1792]{0,1:T(8,128)(2,1)S(1)}, u32[]{:S(2)}, u32[]{:S(2)}) collective-permute-start(bf16[128,1792]{0,1:T(8,128)(2,1)S(1)} %fusion.25), channel_id=1, source_target_pairs={{0,2},{1,3},{2,0},{3,1},{4,6},{5,7},{6,4},{7,5},{8,10},{9,11},{10,... | collective-permute-start | bytes 1376264 | tf_op jit(solution)/shard_map/ppermute | solution.py:15
  206.2 20.6 %collective-permute-done.5 = bf16[128,1792]{0,1:T(8,128)(2,1)S(1)} collective-permute-done((bf16[128,1792]{0,1:T(8,128)(2,1)S(1)}, bf16[128,1792]{0,1:T(8,128)(2,1)S(1)}, u32[]{:S(2)}, u32[]{:S(2)}) %collective-permute-start.5) | collective-permute-done | bytes 458784 | tf_op jit(solution)/shard_map/ppermute | solution.py:15
  226.8 0.3 fusion.29
  227.1 1.6 collective-permute-start.6
  228.7 9.3 %collective-permute-done.6 = bf16[128,1792]{0,1:T(8,128)(2,1)S(1)} collective-permute-done((bf16[128,1792]{0,1:T(8,128)(2,1)S(1)}, bf16[128,1792]{0,1:T(8,128)(2,1)S(1)}, u32[]{:S(2)}, u32[]{:S(2)}) %collective-permute-start.6) | collective-permute-done | bytes 458784 | tf_op jit(solution)/shard_map/ppermute | solution.py:15
  238.0 0.4 fusion.26
  238.4 0.0 copy-start.7
  238.4 3.3 collective-permute-start.7
  241.7 0.0 copy-done.3
  241.7 0.3 copy.21
  242.0 0.0 copy-done.5
  242.0 0.3 copy.22
  242.2 0.0 copy-start.6
  242.3 7.9 %collective-permute-done.7 = bf16[128,1792]{0,1:T(8,128)(2,1)} collective-permute-done((bf16[128,1792]{0,1:T(8,128)(2,1)S(1)}, bf16[128,1792]{0,1:T(8,128)(2,1)}, u32[]{:S(2)}, u32[]{:S(2)}) %collective-permute-start.7) | collective-permute-done | bytes 458784 | tf_op jit(solution)/shard_map/ppermute | solution.py:15
  250.2 1.7 fusion.18
  251.8 0.5 copy.26
  252.4 1.0 convolution_bitcast_fusion
  253.4 0.0 copy-done.6
  253.4 1.2 fusion.23
  254.6 1.4 multiply_convert_fusion
  256.0 1.6 fusion.32
  257.7 1.7 convolution_bitcast_fusion.1
  259.3 0.4 copy.25
  259.8 0.1 collective-permute-start
  259.9 19.6 %collective-permute-done = bf16[128,1792]{0,1:T(8,128)(2,1)S(1)} collective-permute-done((bf16[128,1792]{0,1:T(8,128)(2,1)S(1)}, bf16[128,1792]{0,1:T(8,128)(2,1)S(1)}, u32[]{:S(2)}, u32[]{:S(2)}) %collective-permute-start) | collective-permute-done | bytes 458784 | tf_op jit(solution)/shard_map/ppermute | solution.py:15
  279.5 0.2 fusion.28
  279.7 4.2 collective-permute-start.1
  283.9 16.9 %collective-permute-done.1 = bf16[128,1792]{0,1:T(8,128)(2,1)S(1)} collective-permute-done((bf16[128,1792]{0,1:T(8,128)(2,1)S(1)}, bf16[128,1792]{0,1:T(8,128)(2,1)S(1)}, u32[]{:S(2)}, u32[]{:S(2)}) %collective-permute-start.1) | collective-permute-done | bytes 458784 | tf_op jit(solution)/shard_map/ppermute | solution.py:15
  300.8 0.3 fusion.30
  301.0 1.6 collective-permute-start.2
  302.6 7.7 %collective-permute-done.2 = bf16[128,1792]{0,1:T(8,128)(2,1)S(1)} collective-permute-done((bf16[128,1792]{0,1:T(8,128)(2,1)S(1)}, bf16[128,1792]{0,1:T(8,128)(2,1)S(1)}, u32[]{:S(2)}, u32[]{:S(2)}) %collective-permute-start.2) | collective-permute-done | bytes 458784 | tf_op jit(solution)/shard_map/ppermute | solution.py:15
  310.3 0.2 fusion.27
  310.5 3.8 collective-permute-start.3
  314.3 8.0 %collective-permute-done.3 = bf16[128,1792]{0,1:T(8,128)(2,1)S(1)} collective-permute-done((bf16[128,1792]{0,1:T(8,128)(2,1)S(1)}, bf16[128,1792]{0,1:T(8,128)(2,1)S(1)}, u32[]{:S(2)}, u32[]{:S(2)}) %collective-permute-start.3) | collective-permute-done | bytes 458784 | tf_op jit(solution)/shard_map/ppermute | solution.py:15
  322.2 1.1 fusion.13
  323.3 0.0 all-gather.3.cloned.1.call-update
  323.3 0.0 copy-start.2
  323.4 0.3 reduce-scatter.5.cloned.1.call-start
  323.6 76.3 %all-gather.3.cloned.1.call-done = bf16[2048,1792]{0,1:T(8,128)(2,1)} async-done(((bf16[128,1792]{0,1:T(8,128)(2,1)}), bf16[2048,1792]{0,1:T(8,128)(2,1)}) %all-gather.3.cloned.1.call-update) | async-done | bytes 7340048 | tf_op jit(solution)/shard_map/all_gather | solution.py:67
  399.9 0.0 copy-done.1
  399.9 8.6 %convolution_convert_fusion.1 = bf16[2048,512]{1,0:T(8,128)(2,1)} fusion(bf16[2048,1792]{0,1:T(8,128)(2,1)} %all-gather.3.cloned.1.call-done, bf16[1792,512]{1,0:T(8,128)(2,1)S(1)} %copy-done.1), kind=kOutput, calls=%fused_computation.7 | convolution fusion | flops 3759144960 | bytes 11272192 | tf_op jit(solution)/shard_map/dot_general | solution.py:70
  408.5 0.0 reduce-scatter.5.cloned.1.call-update
  408.5 1.0 copy.30
  409.5 1.0 copy.31
  410.5 10.7 %subtract_multiply_fusion = f32[1792,512]{1,0:T(8,128)} fusion(f32[1792,512]{1,0:T(8,128)} %get-tuple-element.14, bf16[2048,1792]{0,1:T(8,128)(2,1)} %all-gather.3.cloned.1.call-done, bf16[2048,512]{1,0:T(8,128)(2,1)} %all-gather.5.cloned.1.call-done), kind=kOutput, calls=%fused_computation.6 | convolution fusion | flops 3760848896 | bytes 16777216 | tf_op jit(solution)/shard_map/dot_general | solution.py:76
  421.2 72.7 %reduce-scatter.5.cloned.1.call-done = bf16[128,512]{1,0:T(8,128)(2,1)} async-done(((bf16[2048,512]{1,0:T(8,128)(2,1)}), bf16[128,512]{1,0:T(8,128)(2,1)}) %reduce-scatter.5.cloned.1.call-update) | async-done | bytes 131088 | tf_op jit(solution)/shard_map/reduce_scatter | solution.py:69
  (10 shorter events, 0.1 us)
Async XLA Ops:
  7.2 65.4 %all-gather.5.cloned.1.call-start = ((), (), s32[]{:S(2)}) async-start(), calls=%async_computation.4 | async-start | bytes 2228224 | tf_op jit(solution)/shard_map/all_gather | solution.py:75
  7.9 168.5 %reduce-scatter.7.cloned.1.call-start = ((), (), s32[]{:S(2)}) async-start(), calls=%async_computation.5 | async-start | bytes 7798784
  12.9 67.4 %copy-start = (bf16[1792,512]{1,0:T(8,128)(2,1)}, bf16[1792,512]{1,0:T(8,128)(2,1)S(1)}, u32[]{:S(2)}) copy-start(bf16[1792,512]{1,0:T(8,128)(2,1)S(1)} %get-tuple-element.15) | copy-start | bytes 5505028
  90.4 151.3 %copy-start.4 = (bf16[128,1792]{1,0:T(8,128)(2,1)S(1)}, bf16[128,1792]{1,0:T(8,128)(2,1)}, u32[]{:S(2)}) copy-start(bf16[128,1792]{1,0:T(8,128)(2,1)} %param.8) | copy-start | bytes 1376260
  90.4 151.6 %copy-start.5 = (bf16[128,1792]{1,0:T(8,128)(2,1)S(1)}, bf16[128,1792]{1,0:T(8,128)(2,1)}, u32[]{:S(2)}) copy-start(bf16[128,1792]{1,0:T(8,128)(2,1)} %param.9) | copy-start | bytes 1376260
  90.4 309.5 %all-gather.3.cloned.1.call-start = ((), (), s32[]{:S(2)}) async-start(), calls=%async_computation.2 | async-start | bytes 7798784 | tf_op jit(solution)/shard_map/all_gather | solution.py:67
  177.7 23.3 %collective-permute-start.4 = (bf16[128,1792]{0,1:T(8,128)(2,1)S(1)}, bf16[128,1792]{0,1:T(8,128)(2,1)S(1)}, u32[]{:S(2)}, u32[]{:S(2)}) collective-permute-start(bf16[128,1792]{0,1:T(8,128)(2,1)S(1)} %copy.38), channel_id=1, source_target_pairs={{0,1},{1,0},{2,3},{3,2},{4,5},{5,4},{6,7},{7,6},{8,9},{9,8},{10,11... | collective-permute-start | bytes 1376264 | tf_op jit(solution)/shard_map/ppermute | solution.py:15
  180.3 61.9 %copy-start.8 = (s32[1792]{0:T(1024)S(1)}, s32[1792]{0:T(1024)}, u32[]{:S(2)}) copy-start(s32[1792]{0:T(1024)} %param.12) | copy-start | bytes 21508
  201.2 25.6 %collective-permute-start.5 = (bf16[128,1792]{0,1:T(8,128)(2,1)S(1)}, bf16[128,1792]{0,1:T(8,128)(2,1)S(1)}, u32[]{:S(2)}, u32[]{:S(2)}) collective-permute-start(bf16[128,1792]{0,1:T(8,128)(2,1)S(1)} %fusion.25), channel_id=1, source_target_pairs={{0,2},{1,3},{2,0},{3,1},{4,6},{5,7},{6,4},{7,5},{8,10},{9,11},{10,... | collective-permute-start | bytes 1376264 | tf_op jit(solution)/shard_map/ppermute | solution.py:15
  227.1 10.8 %collective-permute-start.6 = (bf16[128,1792]{0,1:T(8,128)(2,1)S(1)}, bf16[128,1792]{0,1:T(8,128)(2,1)S(1)}, u32[]{:S(2)}, u32[]{:S(2)}) collective-permute-start(bf16[128,1792]{0,1:T(8,128)(2,1)S(1)} %fusion.29), channel_id=1, source_target_pairs={{0,4},{1,5},{2,6},{3,7},{4,0},{5,1},{6,2},{7,3},{8,12},{9,13},{10,... | collective-permute-start | bytes 1376264 | tf_op jit(solution)/shard_map/ppermute | solution.py:15
  238.0 3.7 copy-start.3
  238.4 13.9 %copy-start.7 = (f32[14,14,1]{0,1,2:T(8,128)S(1)}, f32[14,14,1]{0,1,2:T(8,128)}, u32[]{:S(2)}) copy-start(f32[14,14,1]{0,1,2:T(8,128)} %constant.35) | copy-start | bytes 2356
  238.4 11.7 %collective-permute-start.7 = (bf16[128,1792]{0,1:T(8,128)(2,1)S(1)}, bf16[128,1792]{0,1:T(8,128)(2,1)}, u32[]{:S(2)}, u32[]{:S(2)}) collective-permute-start(bf16[128,1792]{0,1:T(8,128)(2,1)S(1)} %fusion.26), channel_id=1, source_target_pairs={{0,8},{1,9},{2,10},{3,11},{4,12},{5,13},{6,14},{7,15},{8,0},{9,1},... | collective-permute-start | bytes 1376264 | tf_op jit(solution)/shard_map/ppermute | solution.py:15
  242.2 11.2 %copy-start.6 = (f32[128,128,1]{1,0,2:T(8,128)S(1)}, f32[128,128,1]{1,0,2:T(8,128)}, u32[]{:S(2)}) copy-start(f32[128,128,1]{1,0,2:T(8,128)} %constant.34) | copy-start | bytes 196612
  259.8 19.7 %collective-permute-start = (bf16[128,1792]{0,1:T(8,128)(2,1)S(1)}, bf16[128,1792]{0,1:T(8,128)(2,1)S(1)}, u32[]{:S(2)}, u32[]{:S(2)}) collective-permute-start(bf16[128,1792]{0,1:T(8,128)(2,1)S(1)} %bitcast_convert_fusion), channel_id=1, source_target_pairs={{0,1},{1,0},{2,3},{3,2},{4,5},{5,4},{6,7},{7,6},{8,9},{9,8},{10,11... | collective-permute-start | bytes 1376264 | tf_op jit(solution)/shard_map/ppermute | solution.py:15
  279.7 120.3 %copy-start.1 = (bf16[1792,512]{1,0:T(8,128)(2,1)S(1)}, bf16[1792,512]{1,0:T(8,128)(2,1)}, u32[]{:S(2)}) copy-start(bf16[1792,512]{1,0:T(8,128)(2,1)} %copy-done) | copy-start | bytes 5505028
  279.7 21.1 %collective-permute-start.1 = (bf16[128,1792]{0,1:T(8,128)(2,1)S(1)}, bf16[128,1792]{0,1:T(8,128)(2,1)S(1)}, u32[]{:S(2)}, u32[]{:S(2)}) collective-permute-start(bf16[128,1792]{0,1:T(8,128)(2,1)S(1)} %fusion.28), channel_id=1, source_target_pairs={{0,2},{1,3},{2,0},{3,1},{4,6},{5,7},{6,4},{7,5},{8,10},{9,11},{10,... | collective-permute-start | bytes 1376264 | tf_op jit(solution)/shard_map/ppermute | solution.py:15
  301.0 9.2 %collective-permute-start.2 = (bf16[128,1792]{0,1:T(8,128)(2,1)S(1)}, bf16[128,1792]{0,1:T(8,128)(2,1)S(1)}, u32[]{:S(2)}, u32[]{:S(2)}) collective-permute-start(bf16[128,1792]{0,1:T(8,128)(2,1)S(1)} %get-tuple-element.12), channel_id=1, source_target_pairs={{0,4},{1,5},{2,6},{3,7},{4,0},{5,1},{6,2},{7,3},{8,12},{9,13},{10,... | collective-permute-start | bytes 1376264 | tf_op jit(solution)/shard_map/ppermute | solution.py:15
  310.5 11.8 %collective-permute-start.3 = (bf16[128,1792]{0,1:T(8,128)(2,1)S(1)}, bf16[128,1792]{0,1:T(8,128)(2,1)S(1)}, u32[]{:S(2)}, u32[]{:S(2)}) collective-permute-start(bf16[128,1792]{0,1:T(8,128)(2,1)S(1)} %fusion.27), channel_id=1, source_target_pairs={{0,8},{1,9},{2,10},{3,11},{4,12},{5,13},{6,14},{7,15},{8,0},{9,1},... | collective-permute-start | bytes 1376264 | tf_op jit(solution)/shard_map/ppermute | solution.py:15
  323.3 85.2 %copy-start.2 = (bf16[128,1792]{0,1:T(8,128)(2,1)S(1)}, bf16[128,1792]{0,1:T(8,128)(2,1)}, u32[]{:S(2)}) copy-start(bf16[128,1792]{0,1:T(8,128)(2,1)} %get-tuple-element.17) | copy-start | bytes 1376260
  323.4 170.5 %reduce-scatter.5.cloned.1.call-start = ((), (), s32[]{:S(2)}) async-start(), calls=%async_computation.3 | async-start | bytes 2228224 | tf_op jit(solution)/shard_map/reduce_scatter | solution.py:69
Sparse Core Ops, SparseCore 0:
  10.4 62.1 all-gather.4
  90.5 85.8 reduce-scatter.6
  323.5 76.4 all-gather.2
  408.6 85.1 reduce-scatter.4
where the time goes:
time: 501 us; the launch traced here: 500 us
  waiting for transfers between devices  406 us (81%)
  matrix products  32.4 us (6%)
  starting transfers between devices  22.5 us (4%)
  local copies, waits for them, and re-layouts  14.7 us (3%)
  between operations  14 us (3%)
  other arithmetic  10.7 us (2%)
    ppermute x8, waiting for transfers between devices, partner_2(): lax.ppermute(array, axis, [(i, i ^ 1 << distance) for i in range(lax.axis...  111 us
    unnamed x5, waiting for transfers between devices  86.7 us
    all_gather x1, waiting for transfers between devices, on_device(): all_rows = lax.all_gather(rotated, 'dp', axis=0, tiled=True)  76.3 us
    reduce_scatter x1, waiting for transfers between devices, on_device(): lax.psum_scatter(jnp.dot(piece, weight_q, preferred_element_type=jnp.floa...  72.7 us
    all_gather x1, waiting for transfers between devices, on_device(): grad_all = lax.all_gather(out_grad, 'tensor', axis=0, tiled=True)  59.7 us
    ppermute x8, starting transfers between devices, partner_2(): lax.ppermute(array, axis, [(i, i ^ 1 << distance) for i in range(lax.axis...  22.1 us
    unnamed x24, local copies, waits for them, and re-layouts  13.8 us
    dot_general x1, matrix products, on_device(): lax.dot_general(all_rows, grad_all, (((0,), (0,)), ((), ())), preferred_e...  10.7 us
  transfers between devices with their start and end apart: 12, of which 12 were waited for; matrix products, arithmetic and copies ran while one was open for 4% of the time, Pallas kernels for 0%

commit v1 on v0

v1 whole, which is shorter than its diff:
```python
import jax
import jax.numpy as jnp
import ml_dtypes
import numpy as np
from jax import lax
from jax.experimental import pallas as pl
from jax.experimental.pallas import tpu as pltpu
from jax.sharding import PartitionSpec as P

ROWS = 128
WIDTH = 1792
FEAT = 512
WALSH = 128
COS = 14
HALF = 896
F32 = jnp.float32
BF16 = jnp.bfloat16
MESH = pl.DeviceIdType.MESH

COSINE = np.sqrt(2.0 / COS) * np.cos(
    np.pi * (2 * np.arange(COS)[:, None] + 1) * np.arange(COS)[None, :] / (2.0 * COS)
)
COSINE[:, 0] = np.sqrt(1.0 / COS)
COSINE = COSINE / np.sqrt(WALSH)


def walsh_signs(order):
    a = np.arange(order)[:, None] & np.arange(order)[None, :]
    parity = np.zeros((order, order), np.int64)
    for bit in range(order.bit_length()):
        parity = parity + (a >> bit & 1)
    return (1.0 - 2.0 * (parity % 2)).astype(ml_dtypes.bfloat16)


def walsh_16(src, dst):
    @pl.loop(0, HALF // 128)
    def _(ch):
        cols = pl.ds(pl.multiple_of(ch * 128, 128), 128)
        v = [src[k, :, cols].astype(F32) for k in range(16)]
        for bit in range(4):
            step = 1 << bit
            w = list(v)
            for k in range(16):
                if not k & step:
                    w[k] = v[k] + v[k + step]
                    w[k + step] = v[k] - v[k + step]
            v = w
        for k in range(16):
            dst[k, :, cols] = (v[k] * 0.25).astype(BF16)


def nt(a, b):
    return lax.dot_general(a, b, (((1,), (1,)), ((), ())), preferred_element_type=F32)


def tn(a, b):
    return lax.dot_general(a, b, (((0,), (0,)), ((), ())), preferred_element_type=F32)


def kernel(
    gate, up, w, ex, sg, g, hw,
    lo_out, gd_out, gg_out, gu_out,
    hs, r1, s2, r2, hb, r3, s4, r4, uu,
    gall, wq, dsq, rot,
    pbuf, rsa, rsb, zsnd, zrcv,
    lo, ta, tb, lz, tc, td,
    a_s, a_r, g_s, g_r, c_s, c_r, p_s, p_r, k_s, k_r, t_s, t_r,
):
    dp = lax.axis_index("dp")
    t = lax.axis_index("tensor")
    x, zl, c = dp // 4, (dp // 2) % 2, dp % 2
    y, zh = t // 4, t % 4
    xp, xm, xo = (x + 1) % 4, (x + 3) % 4, (x + 2) % 4
    yp, ym, yo = (y + 1) % 4, (y + 3) % 4, (y + 2) % 4
    hp, hm, ho = (zh + 1) % 4, (zh + 3) % 4, (zh + 2) % 4
    zo, co = 1 - zl, 1 - c
    to_xp = (xp * 4 + zl * 2 + c, t)
    to_xm = (xm * 4 + zl * 2 + c, t)
    to_zl = (x * 4 + zo * 2 + c, t)
    to_co = (x * 4 + zl * 2 + co, t)
    to_yp, to_ym = (dp, yp * 4 + zh), (dp, ym * 4 + zh)
    to_hp, to_hm = (dp, y * 4 + hp), (dp, y * 4 + hm)

    def copy(src, dst, ss, rs, dev):
        return pltpu.make_async_remote_copy(
            src_ref=src, dst_ref=dst, send_sem=ss, recv_sem=rs, device_id=dev, device_id_type=MESH
        )

    sent = []

    def send(src, dst, ss, rs, dev):
        d = copy(src, dst, ss, rs, dev)
        d.start()
        sent.append(d)

    def arrived(dst, ss, rs, dev):
        copy(dst, dst, ss, rs, dev).wait_recv()

    barrier = pltpu.get_barrier_semaphore()

    @pl.loop(1, 16)
    def _(j):
        pl.semaphore_signal(barrier, inc=1, device_id=(dp, (t + j) % 16), device_id_type=MESH)

    for dev in (to_xp, to_xm, to_zl, to_co):
        pl.semaphore_signal(barrier, inc=1, device_id=dev, device_id_type=MESH)

    sign = 2.0 * sg[...].astype(F32) - 1.0

    @pl.loop(0, 8)
    def _(i):
        rows = pl.ds(pl.multiple_of(i * 16, 16), 16)
        v = gate[rows, :].astype(F32)
        h = (v * jax.nn.sigmoid(v) * up[rows, :].astype(F32)).astype(BF16).astype(F32)
        h = (h * sign).astype(BF16)
        hs[2 * i] = h[:, :HALF]
        hs[2 * i + 1] = h[:, HALF:]

    pl.semaphore_wait(barrier, 19)

    def gblk(core, yy, hh):
        return gall.at[core, hh % 2, yy * 2 + hh // 2]

    def ghalf(core, yy, hh, top):
        return gall.at[core, hh % 2, yy * 2 + hh // 2, pl.ds(0 if top else 64, 64)]

    zs = (zh, hm, hp, ho)

    def g_y1(j):
        b = gblk(c, y, zs[j])
        send(b, b, g_s.at[4 + 2 * j], g_r.at[4 + 2 * j], to_yp)
        send(b, b, g_s.at[5 + 2 * j], g_r.at[5 + 2 * j], to_ym)

    def g_y2(j):
        arrived(gblk(c, ym, zs[j]), g_s.at[4 + 2 * j], g_r.at[4 + 2 * j], to_ym)
        b = ghalf(c, ym, zs[j], True)
        send(b, b, g_s.at[12 + 2 * j], g_r.at[12 + 2 * j], to_yp)
        arrived(gblk(c, yp, zs[j]), g_s.at[5 + 2 * j], g_r.at[5 + 2 * j], to_yp)
        b = ghalf(c, yp, zs[j], False)
        send(b, b, g_s.at[13 + 2 * j], g_r.at[13 + 2 * j], to_ym)

    gall[c, zh % 2, y * 2 + zh // 2] = g[...]
    own = gblk(c, y, zh)
    send(own, own, g_s.at[0], g_r.at[0], to_hp)
    send(own, own, g_s.at[1], g_r.at[1], to_hm)
    g_y1(0)

    def a2a_start(src, dst, n):
        @pl.loop(1, 16)
        def _(j):
            d = (t + j) % 16
            copy(src.at[d], dst.at[t], a_s.at[n, j], a_r.at[n, j], (dp, d)).start()

    def a2a_wait(src, dst, n):
        dst[t] = src[t]

        @pl.loop(1, 16)
        def _(j):
            d = (t + 16 - j) % 16
            copy(src.at[d], dst.at[d], a_s.at[n, j], a_r.at[n, j], (dp, d)).wait()

    a2a_start(hs, r1, 0)

    @pl.loop(0, 14)
    def _(i):
        scale = 7.0 * jnp.exp2(ex[pl.ds(i, 1), :].astype(F32))
        inv = 1.0 / scale
        for half in range(2):
            rows = pl.ds(pl.multiple_of(i * 128 + half * 64, 64), 64)
            s = jnp.tanh(w[rows, :].astype(F32) * inv)
            wq[c, rows, :] = (scale * s).astype(BF16)
            dsq[rows, :] = 1.0 - s * s

    send(wq.at[c], wq.at[c], c_s.at[0], c_r.at[0], to_co)

    arrived(gblk(c, y, hm), g_s.at[0], g_r.at[0], to_hm)
    b = ghalf(c, y, hm, True)
    send(b, b, g_s.at[2], g_r.at[2], to_hp)
    g_y1(1)
    arrived(gblk(c, y, hp), g_s.at[1], g_r.at[1], to_hp)
    b = ghalf(c, y, hp, False)
    send(b, b, g_s.at[3], g_r.at[3], to_hm)
    g_y1(2)
    g_y2(0)
    arrived(ghalf(c, y, ho, True), g_s.at[2], g_r.at[2], to_hm)
    arrived(ghalf(c, y, ho, False), g_s.at[3], g_r.at[3], to_hp)
    g_y1(3)
    g_y2(1)
    g_y2(2)

    a2a_wait(hs, r1, 0)
    walsh_16(r1, s2)
    a2a_start(s2, r2, 1)

    g_y2(3)
    for j in range(4):
        arrived(ghalf(c, yo, zs[j], True), g_s.at[12 + 2 * j], g_r.at[12 + 2 * j], to_ym)
        arrived(ghalf(c, yo, zs[j], False), g_s.at[13 + 2 * j], g_r.at[13 + 2 * j], to_yp)

    b = gall.at[c, co]
    send(b, b, c_s.at[1], c_r.at[1], to_co)
    arrived(wq.at[co], c_s.at[0], c_r.at[0], to_co)
    arrived(gall.at[co, c], c_s.at[1], c_r.at[1], to_co)

    def partial(slot, xq):
        a0 = gall[0, c, pl.ds(2 * xq, 2)].reshape(256, FEAT)
        a1 = gall[1, c, pl.ds(2 * xq, 2)].reshape(256, FEAT)
        for n in range(7):
            cols = slice(n * 256, (n + 1) * 256)
            p = nt(a0, wq[0, cols, :]) + nt(a1, wq[1, cols, :])
            pbuf[slot, :, :, cols] = p.astype(BF16).reshape(2, ROWS, 256)

    def add_into(slot, z, src):
        @pl.loop(0, 8)
        def _(i):
            rows = pl.ds(pl.multiple_of(i * 16, 16), 16)
            pbuf[slot, z, rows, :] = (
                pbuf[slot, z, rows, :].astype(F32) + src[rows, :].astype(F32)
            ).astype(BF16)

    partial(2, xo)
    send(pbuf.at[2, zl], rsa.at[0], p_s.at[0], p_r.at[0], to_xp)
    send(pbuf.at[2, zo], rsa.at[1], p_s.at[1], p_r.at[1], to_xm)
    partial(1, xp)
    send(pbuf.at[1, zo], rsb.at[0, 0], p_s.at[2], p_r.at[2], to_xp)
    partial(3, xm)
    send(pbuf.at[3, zl], rsb.at[1, 1], p_s.at[3], p_r.at[3], to_xm)
    partial(0, x)

    def local_walsh(src):
        for m in range(COS):
            j, k = m // 7, m % 7
            blk = jnp.concatenate([src[2 * i + j, :, 128 * k:128 * k + 128] for i in range(8)], axis=0)
            uu[m] = jnp.dot(blk, hw[...], preferred_element_type=F32)

    a2a_wait(s2, r2, 1)
    local_walsh(r2)
    me = 2 * x + zl

    @pl.loop(0, 8)
    def _(i):
        rows = pl.ds(pl.multiple_of(i * 16, 16), 16)
        u = [uu[m, rows, :] for m in range(COS)]
        ev = [u[m] + u[13 - m] for m in range(7)]
        od = [u[m] - u[13 - m] for m in range(7)]
        for n in range(COS):
            part = od if n % 2 else ev
            acc = part[0] * float(COSINE[0, n])
            for m in range(1, 7):
                acc = acc + part[m] * float(COSINE[m, n])
            rot[c, me, rows, 128 * n:128 * n + 128] = acc.astype(BF16)

    def rblk(xx, zz, cc):
        return rot.at[cc, 2 * xx + zz]

    def to_sibling(n, xx, zz):
        b = rblk(xx, zz, c)
        send(b, b, k_s.at[7 + n], k_r.at[7 + n], to_co)

    def gather(n, xx, zz, dev):
        b = rblk(xx, zz, c)
        send(b, b, k_s.at[n], k_r.at[n], dev)

    def gathered(n, xx, zz, dev):
        arrived(rblk(xx, zz, c), k_s.at[n], k_r.at[n], dev)

    gather(0, x, zl, to_zl)
    to_sibling(0, x, zl)

    arrived(rsa.at[0], p_s.at[0], p_r.at[0], to_xm)
    add_into(1, zl, rsa.at[0])
    send(pbuf.at[1, zl], rsb.at[0, 1], p_s.at[4], p_r.at[4], to_xp)
    arrived(rsa.at[1], p_s.at[1], p_r.at[1], to_xp)
    add_into(3, zo, rsa.at[1])
    send(pbuf.at[3, zo], rsb.at[1, 0], p_s.at[5], p_r.at[5], to_xm)

    gather(1, x, zl, to_xp)
    gather(4, x, zl, to_xm)
    gathered(0, x, zo, to_zl)
    gather(2, x, zo, to_xp)
    gather(5, x, zo, to_xm)
    to_sibling(1, x, zo)

    arrived(rsb.at[0, 0], p_s.at[2], p_r.at[2], to_xm)
    arrived(rsb.at[1, 0], p_s.at[5], p_r.at[5], to_xp)

    @pl.loop(0, 8)
    def _(i):
        rows = pl.ds(pl.multiple_of(i * 16, 16), 16)
        zsnd[rows, :] = (
            pbuf[0, zo, rows, :].astype(F32)
            + rsb[0, 0, rows, :].astype(F32)
            + rsb[1, 0, rows, :].astype(F32)
        ).astype(BF16)

    send(zsnd, zrcv, p_s.at[6], p_r.at[6], to_zl)

    arrived(rsb.at[0, 1], p_s.at[4], p_r.at[4], to_xm)
    arrived(rsb.at[1, 1], p_s.at[3], p_r.at[3], to_xp)
    arrived(zrcv, p_s.at[6], p_r.at[6], to_zl)

    @pl.loop(0, 8)
    def _(i):
        rows = pl.ds(pl.multiple_of(i * 16, 16), 16)
        s = (
            pbuf[0, zl, rows, :].astype(F32)
            + rsb[0, 1, rows, :].astype(F32)
            + rsb[1, 1, rows, :].astype(F32)
            + zrcv[rows, :].astype(F32)
        ).astype(BF16)
        hb[2 * i] = s[:, :HALF]
        hb[2 * i + 1] = s[:, HALF:]

    a2a_start(hb, r3, 2)

    gathered(1, xm, zl, to_xm)
    gather(3, xm, zl, to_xp)
    to_sibling(2, xm, zl)
    gathered(4, xp, zl, to_xp)
    to_sibling(3, xp, zl)
    gathered(5, xp, zo, to_xp)
    gather(6, xp, zo, to_xm)
    to_sibling(4, xp, zo)
    gathered(2, xm, zo, to_xm)
    to_sibling(5, xm, zo)

    a2a_wait(hb, r3, 2)
    walsh_16(r3, s4)
    a2a_start(s4, r4, 3)

    def project(yq):
        for par in range(2):
            a = rot[par, pl.ds(2 * yq, 2)].reshape(256, WIDTH)
            for n in range(2):
                cols = slice(n * 256, n * 256 + 256)
                p = jnp.dot(a, wq[c, :, cols], preferred_element_type=F32)
                lo[yq, par, :, :, cols] = p.astype(BF16).reshape(2, ROWS, 256)

    gathered(3, xo, zl, to_xm)
    to_sibling(6, xo, zl)
    gathered(6, xo, zo, to_xp)
    to_sibling(7, xo, zo)

    for n, (xx, zz) in enumerate(
        ((x, zl), (x, zo), (xm, zl), (xp, zl), (xp, zo), (xm, zo), (xo, zl), (xo, zo))
    ):
        arrived(rblk(xx, zz, co), k_s.at[7 + n], k_r.at[7 + n], to_co)

    project(yo)
    send(lo.at[yo, 0], ta.at[0], t_s.at[0], t_r.at[0], to_yp)
    send(lo.at[yo, 1], ta.at[1], t_s.at[1], t_r.at[1], to_ym)
    project(yp)
    send(lo.at[yp, 1], tb.at[0, 1], t_s.at[2], t_r.at[2], to_yp)
    project(ym)
    send(lo.at[ym, 0], tb.at[1, 0], t_s.at[3], t_r.at[3], to_ym)

    arrived(ta.at[0], t_s.at[0], t_r.at[0], to_ym)
    lo[yp, 0] = (lo[yp, 0].astype(F32) + ta[0].astype(F32)).astype(BF16)
    send(lo.at[yp, 0], tb.at[0, 0], t_s.at[4], t_r.at[4], to_yp)
    arrived(ta.at[1], t_s.at[1], t_r.at[1], to_yp)
    lo[ym, 1] = (lo[ym, 1].astype(F32) + ta[1].astype(F32)).astype(BF16)
    send(lo.at[ym, 1], tb.at[1, 1], t_s.at[5], t_r.at[5], to_ym)
    project(y)

    def down(lo_n, hi_n):
        @pl.loop(lo_n, hi_n)
        def _(n):
            cols = pl.ds(pl.multiple_of(n * 256, 256), 256)
            acc = None
            for par in range(2):
                for q in range(2):
                    a = rot[par, 4 * q:4 * q + 4, :, cols].reshape(512, 256)
                    p = tn(a, gall[c, par, 4 * q:4 * q + 4].reshape(512, FEAT))
                    acc = p if acc is None else acc + p
            gd_out[cols, :] = acc * dsq[cols, :]

    down(0, 4)

    for par in range(2):
        i = 2 + 2 * par
        arrived(tb.at[0, 1 - par], t_s.at[i], t_r.at[i], to_ym)
        arrived(tb.at[1, par], t_s.at[i + 1], t_r.at[i + 1], to_yp)
    for par in range(2):
        lz[par] = (
            lo[y, par].astype(F32) + tb[0, par].astype(F32) + tb[1, par].astype(F32)
        ).astype(BF16)

    def lzh(hh, top):
        return lz.at[hh % 2, hh // 2, pl.ds(0 if top else 64, 64)]

    send(lzh(ho, True), tc.at[0], t_s.at[6], t_r.at[6], to_hp)
    send(lzh(ho, False), tc.at[1], t_s.at[7], t_r.at[7], to_hm)
    down(4, 6)
    arrived(tc.at[0], t_s.at[6], t_r.at[6], to_hm)
    v = lzh(hp, True)
    v[...] = (v[...].astype(F32) + tc[0].astype(F32)).astype(BF16)
    b = lz.at[hp % 2, hp // 2]
    send(b, td.at[0], t_s.at[8], t_r.at[8], to_hp)
    arrived(tc.at[1], t_s.at[7], t_r.at[7], to_hp)
    v = lzh(hm, False)
    v[...] = (v[...].astype(F32) + tc[1].astype(F32)).astype(BF16)
    b = lz.at[hm % 2, hm // 2]
    send(b, td.at[1], t_s.at[9], t_r.at[9], to_hm)
    down(6, 7)

    a2a_wait(s4, r4, 3)
    local_walsh(r4)

    @pl.loop(0, 8)
    def _(i):
        rows = pl.ds(pl.multiple_of(i * 16, 16), 16)
        for m in range(7):
            evn = uu[0, rows, :] * float(COSINE[m, 0])
            odd = uu[1, rows, :] * float(COSINE[m, 1])
            for n in range(2, COS, 2):
                evn = evn + uu[n, rows, :] * float(COSINE[m, n])
                odd = odd + uu[n + 1, rows, :] * float(COSINE[m, n + 1])
            for mm, val in ((m, evn + odd), (13 - m, evn - odd)):
                cols = slice(128 * mm, 128 * mm + 128)
                gh = val * sign[:, cols]
                v = gate[rows, cols].astype(F32)
                sigma = jax.nn.sigmoid(v)
                gg_out[rows, cols] = (
                    gh * up[rows, cols].astype(F32) * sigma * (1.0 + v * (1.0 - sigma))
                ).astype(BF16)
                gu_out[rows, cols] = (gh * (v * sigma)).astype(BF16)

    arrived(td.at[0], t_s.at[8], t_r.at[8], to_hm)
    arrived(td.at[1], t_s.at[9], t_r.at[9], to_hp)
    lo_out[...] = (
        lz[zh % 2, zh // 2].astype(F32) + td[0].astype(F32) + td[1].astype(F32)
    ).astype(BF16)

    for d in sent:
        d.wait_send()


def on_device(gate_pre, up_pre, down_rotated, exponents, signs, out_grad):
    vmem = pl.BlockSpec(memory_space=pltpu.VMEM)
    blocks = pltpu.VMEM((16, 16, HALF), BF16)
    dma = pltpu.SemaphoreType.DMA
    return pl.pallas_call(
        kernel,
        out_shape=(
            jax.ShapeDtypeStruct((ROWS, FEAT), BF16),
            jax.ShapeDtypeStruct((WIDTH, FEAT), F32),
            jax.ShapeDtypeStruct((ROWS, WIDTH), BF16),
            jax.ShapeDtypeStruct((ROWS, WIDTH), BF16),
        ),
        in_specs=[vmem] * 7,
        out_specs=(vmem,) * 4,
        scratch_shapes=[blocks] * 8
        + [
            pltpu.VMEM((COS, ROWS, WALSH), F32),
            pltpu.VMEM((2, 2, 8, ROWS, FEAT), BF16),
            pltpu.VMEM((2, WIDTH, FEAT), BF16),
            pltpu.VMEM((WIDTH, FEAT), F32),
            pltpu.VMEM((2, 8, ROWS, WIDTH), BF16),
            pltpu.VMEM((4, 2, ROWS, WIDTH), BF16),
            pltpu.VMEM((2, ROWS, WIDTH), BF16),
            pltpu.VMEM((2, 2, ROWS, WIDTH), BF16),
            pltpu.VMEM((ROWS, WIDTH), BF16),
            pltpu.VMEM((ROWS, WIDTH), BF16),
            pltpu.VMEM((4, 2, 2, ROWS, FEAT), BF16),
            pltpu.VMEM((2, 2, ROWS, FEAT), BF16),
            pltpu.VMEM((2, 2, 2, ROWS, FEAT), BF16),
            pltpu.VMEM((2, 2, ROWS, FEAT), BF16),
            pltpu.VMEM((2, 64, FEAT), BF16),
            pltpu.VMEM((2, ROWS, FEAT), BF16),
            dma((4, 16)), dma((4, 16)),
            dma((20,)), dma((20,)),
            dma((2,)), dma((2,)),
            dma((7,)), dma((7,)),
            dma((15,)), dma((15,)),
            dma((10,)), dma((10,)),
        ],
        compiler_params=pltpu.CompilerParams(
            collective_id=0, has_side_effects=True, vmem_limit_bytes=60 * 1024 * 1024
        ),
        cost_estimate=pl.CostEstimate(
            flops=11_300_000_000, bytes_accessed=9_000_000, transcendentals=2_000_000
        ),
    )(
        gate_pre, up_pre, down_rotated, exponents, signs.reshape(1, WIDTH), out_grad,
        jnp.asarray(walsh_signs(WALSH)),
    )


def solution(mesh):
    return jax.shard_map(
        on_device,
        mesh=mesh,
        in_specs=(
            P("dp", "tensor"),
            P("dp", "tensor"),
            P("tensor", "dp"),
            P("tensor", "dp"),
            P("tensor"),
            P("tensor", "dp"),
        ),
        out_specs=(P("tensor", "dp"), P("tensor", "dp"), P("dp", "tensor"), P("dp", "tensor")),
        check_vma=False,
    )
```

time: 501 us -> 163 us (0.33)
  waiting for transfers between devices: 406 us -> 0 us
  Pallas kernels: 0 us -> 151 us
  matrix products: 32.4 us -> 0 us
  starting transfers between devices: 22.5 us -> 0 us
  between operations: 14 us -> 0.64 us
  other arithmetic: 10.7 us -> 0 us
  local copies, waits for them, and re-layouts: 14.7 us -> 8.73 us
    pallas_call x0 -> x1, Pallas kernels: none -> 151 us  [on_device(): pl.pallas_call(kernel, out_shape=(jax.ShapeDtypeStruct((ROWS, FEAT), BF16...]
    all_gather x2 -> x0, waiting for transfers between devices: 136 us -> none  [the longest x1 76.3 us: on_device(): all_rows = lax.all_gather(rotated, 'dp', axis=0, tiled=True)]
    ppermute x8 -> x0, waiting for transfers between devices: 111 us -> none  [partner_2(): lax.ppermute(array, axis, [(i, i ^ 1 << distance) for i in range(lax.axis...]
    unnamed x5 -> x0, waiting for transfers between devices: 86.7 us -> none
    reduce_scatter x1 -> x0, waiting for transfers between devices: 72.7 us -> none  [on_device(): lax.psum_scatter(jnp.dot(piece, weight_q, preferred_element_type=jnp.floa...]
    dot_general x7 -> x0, matrix products: 32.4 us -> none  [the longest x1 10.7 us: on_device(): lax.dot_general(all_rows, grad_all, (((0,), (0,)), ((), ())), preferred_e...]
    ppermute x8 -> x0, starting transfers between devices: 22.1 us -> none  [partner_2(): lax.ppermute(array, axis, [(i, i ^ 1 << distance) for i in range(lax.axis...]
    unnamed x24 -> x8, local copies, waits for them, and re-layouts: 13.8 us -> 7.44 us
  transfers between devices with their start and end apart: 12 -> 0, of which waited for: 12 -> 0; matrix products, arithmetic and copies ran while one was open for 4% -> 0% of each run, Pallas kernels for 0% -> 0%
where the time goes in v1:
time: 163 us; the launch traced here: 161 us
  Pallas kernels  151 us (93%)
  local copies, waits for them, and re-layouts  8.73 us (5%)
    pallas_call x1, Pallas kernels, on_device(): pl.pallas_call(kernel, out_shape=(jax.ShapeDtypeStruct((ROWS, FEAT), BF16...  151 us
    unnamed x8, local copies, waits for them, and re-layouts  7.44 us

profile of v1, /device:TPU:2, one launch (start us, length us, event | category | flops | bytes accessed | tf_op | source)
XLA Modules:
  0.0 160.7 jit_solution(17499896486834841644)
XLA Ops:
  0.6 1.3 reshape.11.sg
  1.9 151.4 %shard_map.102 = (bf16[128,512]{1,0:T(8,128)(2,1)}, f32[1792,512]{1,0:T(8,128)}, bf16[128,1792]{1,0:T(8,128)(2,1)}, bf16[128,1792]{1,0:T(8,128)(2,1)}) custom-call(bf16[128,1792]{1,0:T(8,128)(2,1)} %gate.1, bf16[128,1792]{1,0:T(8,128)(2,1)} %up.1, bf16[1792,512]{1,0:T(8,128)(2,1)} %w.1, s32[14,512]{1,0:T(8,128)} %ex.1, s32[1,1792]{1,0:T(1,128)} %reshape.11.sg, ...), custom_call_target="tpu_custom_call" | custom-call | flops 11299999744 | bytes 9000000 | tf_op jit(solution)/shard_map/pallas_call | solution.py:442
  153.3 1.6 copy.15
  154.9 0.0 copy-start.1
  154.9 0.0 copy-start
  154.9 4.3 %copy.16 = f32[1792,512]{1,0:T(8,128)} copy(f32[1792,512]{1,0:T(8,128)} %get-tuple-element.9) | data formatting | bytes 7340032
  159.2 0.0 copy-done.1
  159.2 0.8 copy.17
  160.0 0.0 copy-done
  160.0 0.8 copy.18
Async XLA Ops:
  154.9 4.3 %copy-start.1 = (bf16[128,1792]{1,0:T(8,128)(2,1)S(1)}, bf16[128,1792]{1,0:T(8,128)(2,1)}, u32[]{:S(2)}) copy-start(bf16[128,1792]{1,0:T(8,128)(2,1)} %get-tuple-element.10) | copy-start | bytes 1376260
  154.9 5.1 %copy-start = (bf16[128,1792]{1,0:T(8,128)(2,1)S(1)}, bf16[128,1792]{1,0:T(8,128)(2,1)}, u32[]{:S(2)}) copy-start(bf16[128,1792]{1,0:T(8,128)(2,1)} %get-tuple-element.11) | copy-start | bytes 1376260

commit v2 on v0

v2 whole, which is shorter than its diff:
```python
import jax
import jax.numpy as jnp
import ml_dtypes
import numpy as np
from jax import lax
from jax.experimental import pallas as pl
from jax.experimental.pallas import tpu as pltpu
from jax.sharding import PartitionSpec as P

ROWS = 128
WIDTH = 1792
FEAT = 512
WALSH = 128
COS = 14
HALF = 896
WAVES = 4
WR = ROWS // WAVES
F32 = jnp.float32
BF16 = jnp.bfloat16
MESH = pl.DeviceIdType.MESH

COSINE = np.sqrt(2.0 / COS) * np.cos(
    np.pi * (2 * np.arange(COS)[:, None] + 1) * np.arange(COS)[None, :] / (2.0 * COS)
)
COSINE[:, 0] = np.sqrt(1.0 / COS)
COSINE = COSINE / np.sqrt(WALSH)


def walsh_signs(order):
    a = np.arange(order)[:, None] & np.arange(order)[None, :]
    parity = np.zeros((order, order), np.int64)
    for bit in range(order.bit_length()):
        parity = parity + (a >> bit & 1)
    return (1.0 - 2.0 * (parity % 2)).astype(ml_dtypes.bfloat16)


def walsh(order, src, dst):
    scale = 1.0 / np.sqrt(order)
    height, width = src.shape[1:]

    @pl.loop(0, height // 16)
    def _(i):
        rows = pl.ds(pl.multiple_of(i * 16, 16), 16)

        @pl.loop(0, width // 128)
        def _(ch):
            cols = pl.ds(pl.multiple_of(ch * 128, 128), 128)
            v = [src[k, rows, cols].astype(F32) for k in range(order)]
            step = 1
            while step < order:
                w = list(v)
                for k in range(order):
                    if not k & step:
                        w[k] = v[k] + v[k + step]
                        w[k + step] = v[k] - v[k + step]
                v = w
                step *= 2
            for k in range(order):
                dst[k, rows, cols] = (v[k] * scale).astype(BF16)


def nt(a, b):
    return lax.dot_general(a, b, (((1,), (1,)), ((), ())), preferred_element_type=F32)


def tn(a, b):
    return lax.dot_general(a, b, (((0,), (0,)), ((), ())), preferred_element_type=F32)


def kernel(
    gate_h, up_h, w_h, ex_h, sg_h, g_h, hw_h,
    lo_out, gd_out, gg_out, gu_out,
    gate, up, w, ex, sg, hw,
    f0, f1, f2, f3, f4, f5, f6, hb, r3, s4, r4, uu,
    gall, wq, dsq, rot,
    pbuf, rsa, rsb, zsnd, zrcv,
    lo, ta, tb, lz, tc, td,
    lov, gdv, ggv, guv,
    i_s, o_s, f_s, f_r, a_s, a_r, g_s, g_r, c_s, c_r, p_s, p_r, k_s, k_r, t_s, t_r,
):
    dp = lax.axis_index("dp")
    t = lax.axis_index("tensor")
    x, zl, c = dp // 4, (dp // 2) % 2, dp % 2
    y, zh = t // 4, t % 4
    xp, xm, xo = (x + 1) % 4, (x + 3) % 4, (x + 2) % 4
    yp, ym, yo = (y + 1) % 4, (y + 3) % 4, (y + 2) % 4
    hp, hm, ho = (zh + 1) % 4, (zh + 3) % 4, (zh + 2) % 4
    zo, co = 1 - zl, 1 - c
    to_xp = (xp * 4 + zl * 2 + c, t)
    to_xm = (xm * 4 + zl * 2 + c, t)
    to_zl = (x * 4 + zo * 2 + c, t)
    to_co = (x * 4 + zl * 2 + co, t)
    to_yp, to_ym = (dp, yp * 4 + zh), (dp, ym * 4 + zh)
    to_hp, to_hm = (dp, y * 4 + hp), (dp, y * 4 + hm)

    def copy(src, dst, ss, rs, dev):
        return pltpu.make_async_remote_copy(
            src_ref=src, dst_ref=dst, send_sem=ss, recv_sem=rs, device_id=dev, device_id_type=MESH
        )

    sent = []

    def send(src, dst, ss, rs, dev):
        d = copy(src, dst, ss, rs, dev)
        d.start()
        sent.append(d)

    def arrived(dst, ss, rs, dev):
        copy(dst, dst, ss, rs, dev).wait_recv()

    g_in = pltpu.make_async_copy(g_h, gall.at[c, zh % 2, y * 2 + zh // 2], i_s.at[0])
    g_in.start()
    loads = [
        pltpu.make_async_copy(src, dst, i_s.at[1 + n])
        for n, (src, dst) in enumerate(((sg_h, sg), (gate_h, gate), (up_h, up), (ex_h, ex), (w_h, w), (hw_h, hw)))
    ]
    barrier = pltpu.get_barrier_semaphore()

    @pl.loop(1, 16)
    def _(j):
        pl.semaphore_signal(barrier, inc=1, device_id=(dp, (t + j) % 16), device_id_type=MESH)

    for dev in (to_xp, to_xm, to_zl, to_co):
        pl.semaphore_signal(barrier, inc=1, device_id=dev, device_id_type=MESH)
    for d in loads:
        d.start()
    g_in.wait()
    pl.semaphore_wait(barrier, 19)

    def gblk(core, yy, hh):
        return gall.at[core, hh % 2, yy * 2 + hh // 2]

    def ghalf(core, yy, hh, top):
        return gall.at[core, hh % 2, yy * 2 + hh // 2, pl.ds(0 if top else 64, 64)]

    zs = (zh, hm, hp, ho)

    def g_z(n, hh, top, dev):
        b = ghalf(c, y, hh, top)
        send(b, b, g_s.at[n], g_r.at[n], dev)

    def g_zd(n, hh, top, dev):
        arrived(ghalf(c, y, hh, top), g_s.at[n], g_r.at[n], dev)

    def g_y1(j, top):
        n = 6 + 6 * j + (0 if top else 2)
        b = ghalf(c, y, zs[j], top)
        send(b, b, g_s.at[n], g_r.at[n], to_yp)
        send(b, b, g_s.at[n + 1], g_r.at[n + 1], to_ym)

    def g_yd(j, n, yy, top, dev):
        n = 6 + 6 * j + n
        arrived(ghalf(c, yy, zs[j], top), g_s.at[n], g_r.at[n], dev)

    def g_y2(j):
        n = 6 + 6 * j
        g_yd(j, 0, ym, True, to_ym)
        b = ghalf(c, ym, zs[j], True)
        send(b, b, g_s.at[n + 4], g_r.at[n + 4], to_yp)
        g_yd(j, 3, yp, False, to_yp)
        b = ghalf(c, yp, zs[j], False)
        send(b, b, g_s.at[n + 5], g_r.at[n + 5], to_ym)

    def g_core(n, yy):
        b = gall.at[c, co, pl.ds(2 * yy, 2)]
        send(b, b, c_s.at[1 + n], c_r.at[1 + n], to_co)

    def g_cored(n, yy):
        arrived(gall.at[co, c, pl.ds(2 * yy, 2)], c_s.at[1 + n], c_r.at[1 + n], to_co)

    g_z(0, zh, True, to_hp)
    g_z(1, zh, False, to_hm)
    g_y1(0, True)
    g_y1(0, False)
    g_z(2, zh, False, to_hp)
    g_z(3, zh, True, to_hm)

    for d in loads[:3]:
        d.wait()
    sign = jnp.concatenate([sg[pl.ds(128 * m, 128)].reshape(1, 128) for m in range(COS)], axis=1)
    sign = 2.0 * sign.astype(F32) - 1.0

    @pl.loop(0, 8)
    def _(i):
        rows = pl.ds(pl.multiple_of(i * 16, 16), 16)
        v = gate[rows, :].astype(F32)
        h = (v * jax.nn.sigmoid(v) * up[rows, :].astype(F32)).astype(BF16).astype(F32)
        f0[i // 2, pl.ds(pl.multiple_of(i % 2 * 16, 16), 16), :] = (h * sign).astype(BF16)

    def stage_dev(n, d):
        return (dp, y * 4 + d) if n < 2 else (dp, d * 4 + zh)

    def stage_start(src, dst, n):
        me = zh if n < 2 else y
        for j in range(1, 4):
            d = (me + j) % 4
            copy(src.at[d], dst.at[me], f_s.at[n, j], f_r.at[n, j], stage_dev(n, d)).start()

    def stage_wait(src, dst, n):
        me = zh if n < 2 else y
        dst[me] = src[me]
        for j in range(1, 4):
            d = (me + 4 - j) % 4
            copy(src.at[d], dst.at[d], f_s.at[n, j], f_r.at[n, j], stage_dev(n, d)).wait()

    g_zd(0, hm, True, to_hm)
    g_z(4, hm, True, to_hp)
    g_y1(1, True)
    g_zd(1, hp, False, to_hp)
    g_z(5, hp, False, to_hm)
    g_y1(2, False)
    g_y2(0)
    g_zd(2, hm, False, to_hm)
    g_y1(1, False)
    g_zd(3, hp, True, to_hp)
    g_y1(2, True)
    stage_start(f0, f1, 0)

    for d in loads[3:]:
        d.wait()

    @pl.loop(0, 14)
    def _(i):
        scale = 7.0 * jnp.exp2(ex[pl.ds(i, 1), :].astype(F32))
        inv = 1.0 / scale
        for half in range(2):
            rows = pl.ds(pl.multiple_of(i * 128 + half * 64, 64), 64)
            s = jnp.tanh(w[rows, :].astype(F32) * inv)
            wq[c, rows, :] = (scale * s).astype(BF16)
            dsq[rows, :] = 1.0 - s * s

    send(wq.at[c], wq.at[c], c_s.at[0], c_r.at[0], to_co)

    g_zd(4, ho, True, to_hm)
    g_y1(3, True)
    g_zd(5, ho, False, to_hp)
    g_y1(3, False)
    g_core(0, y)
    g_y2(1)
    g_y2(2)

    def a2a_start(src, dst, n):
        @pl.loop(1, 16)
        def _(j):
            d = (t + j) % 16
            copy(src.at[d], dst.at[t], a_s.at[n, j], a_r.at[n, j], (dp, d)).start()

    def a2a_wait(src, dst, n):
        dst[t] = src[t]

        @pl.loop(1, 16)
        def _(j):
            d = (t + 16 - j) % 16
            copy(src.at[d], dst.at[d], a_s.at[n, j], a_r.at[n, j], (dp, d)).wait()

    top, low = pl.ds(0, 64), pl.ds(64, 64)

    def add_into(slot, z, half, src):
        @pl.loop(0, 4)
        def _(i):
            here = pl.ds(pl.multiple_of(i * 16, 16), 16)
            rows = pl.ds(pl.multiple_of(half * 64 + i * 16, 16), 16)
            pbuf[slot, z, rows, :] = (
                pbuf[slot, z, rows, :].astype(F32) + src[here, :].astype(F32)
            ).astype(BF16)

    def p_copy(k, n, src, dst, dev):
        return copy(src, dst, p_s.at[6 * k + n], p_r.at[6 * k + n], dev)

    p_far, p_next, p_last = [], [], []
    for k, z in ((0, zo), (1, zl)):
        p_far.append(p_copy(k, 0, pbuf.at[2, z, top], rsa.at[k, 0], to_xp))
        p_far.append(p_copy(k, 1, pbuf.at[2, z, low], rsa.at[k, 1], to_xm))
        p_next.append(p_copy(k, 2, pbuf.at[1, z, low], rsb.at[k, 0, low], to_xp))
        p_last.append(p_copy(k, 3, pbuf.at[3, z, top], rsb.at[k, 1, top], to_xm))
    sent.extend((*p_far, *p_next, *p_last))

    def p_onward(k, z):
        p_copy(k, 0, rsa.at[k, 0], rsa.at[k, 0], to_xm).wait_recv()
        add_into(1, z, 0, rsa.at[k, 0])
        d = p_copy(k, 4, pbuf.at[1, z, top], rsb.at[k, 0, top], to_xp)
        d.start()
        sent.append(d)
        p_copy(k, 1, rsa.at[k, 1], rsa.at[k, 1], to_xp).wait_recv()
        add_into(3, z, 1, rsa.at[k, 1])
        d = p_copy(k, 5, pbuf.at[3, z, low], rsb.at[k, 1, low], to_xm)
        d.start()
        sent.append(d)

    def p_arrived(k):
        p_copy(k, 2, rsb.at[k, 0, low], rsb.at[k, 0, low], to_xm).wait_recv()
        p_copy(k, 3, rsb.at[k, 1, top], rsb.at[k, 1, top], to_xp).wait_recv()
        p_copy(k, 4, rsb.at[k, 0, top], rsb.at[k, 0, top], to_xm).wait_recv()
        p_copy(k, 5, rsb.at[k, 1, low], rsb.at[k, 1, low], to_xp).wait_recv()

    def partial(n, q):
        g_cored(n, q)
        slot = (q + 4 - x) % 4
        a0 = gall[0, c, pl.ds(2 * q, 2)].reshape(256, FEAT)
        a1 = gall[1, c, pl.ds(2 * q, 2)].reshape(256, FEAT)
        for n in range(7):
            cols = slice(n * 256, (n + 1) * 256)
            p = nt(a0, wq[0, cols, :]) + nt(a1, wq[1, cols, :])
            pbuf[slot, :, :, cols] = p.astype(BF16).reshape(2, ROWS, 256)

        @pl.when(slot == 2)
        def _():
            p_far[0].start()
            p_far[1].start()

        @pl.when(slot == 1)
        def _():
            p_next[0].start()

        @pl.when(slot == 3)
        def _():
            p_last[0].start()

    arrived(wq.at[co], c_s.at[0], c_r.at[0], to_co)
    partial(0, y)
    g_y2(3)
    for j in range(4):
        g_yd(j, 2, ym, False, to_ym)
        g_yd(j, 1, yp, True, to_yp)
    g_core(1, ym)
    g_core(2, yp)
    partial(1, ym)
    partial(2, yp)
    for j in range(4):
        g_yd(j, 4, yo, True, to_ym)
        g_yd(j, 5, yo, False, to_yp)
    g_core(3, yo)
    partial(3, yo)
    stage_wait(f0, f1, 0)
    walsh(4, f1, f2)
    stage_start(f2, f3, 1)
    p_onward(0, zo)
    for d in (p_far[2], p_far[3], p_next[1], p_last[1]):
        d.start()
    stage_wait(f2, f3, 1)
    stage_start(f3, f4, 2)

    p_arrived(0)

    @pl.loop(0, 8)
    def _(i):
        rows = pl.ds(pl.multiple_of(i * 16, 16), 16)
        zsnd[rows, :] = (
            pbuf[0, zo, rows, :].astype(F32)
            + rsb[0, 0, rows, :].astype(F32)
            + rsb[0, 1, rows, :].astype(F32)
        ).astype(BF16)

    send(zsnd, zrcv, p_s.at[12], p_r.at[12], to_zl)
    stage_wait(f3, f4, 2)
    walsh(4, f4, f5)
    stage_start(f5, f6, 3)
    p_onward(1, zl)
    stage_wait(f5, f6, 3)

    def local_walsh(block):
        for m in range(COS):
            uu[m] = jnp.dot(block(m), hw[...], preferred_element_type=F32)

    local_walsh(lambda m: f6[:, :, 128 * m:128 * m + 128].reshape(ROWS, WALSH))
    me = 2 * x + zl

    @pl.loop(0, 8)
    def _(i):
        rows = pl.ds(pl.multiple_of(i * 16, 16), 16)
        u = [uu[m, rows, :] for m in range(COS)]
        ev = [u[m] + u[13 - m] for m in range(7)]
        od = [u[m] - u[13 - m] for m in range(7)]
        for n in range(COS):
            part = od if n % 2 else ev
            acc = part[0] * float(COSINE[0, n])
            for m in range(1, 7):
                acc = acc + part[m] * float(COSINE[m, n])
            rot[c, me, rows, 128 * n:128 * n + 128] = acc.astype(BF16)

    def rblk(h, xx, zz, cc):
        return rot.at[cc, 2 * xx + zz, pl.ds(WR * h, WR)]

    def to_sibling(h, n, xx, zz):
        b = rblk(h, xx, zz, c)
        send(b, b, k_s.at[15 * h + 7 + n], k_r.at[15 * h + 7 + n], to_co)

    def gather(h, n, xx, zz, dev):
        b = rblk(h, xx, zz, c)
        send(b, b, k_s.at[15 * h + n], k_r.at[15 * h + n], dev)

    def gathered(h, n, xx, zz, dev):
        arrived(rblk(h, xx, zz, c), k_s.at[15 * h + n], k_r.at[15 * h + n], dev)

    def gather_zl(h):
        gather(h, 0, x, zl, to_zl)
        to_sibling(h, 0, x, zl)

    def gather_own(h):
        gather(h, 1, x, zl, to_xp)
        gather(h, 4, x, zl, to_xm)

    def gather_partner(h):
        gathered(h, 0, x, zo, to_zl)
        gather(h, 2, x, zo, to_xp)
        gather(h, 5, x, zo, to_xm)
        to_sibling(h, 1, x, zo)

    def gather_on(h):
        gathered(h, 1, xm, zl, to_xm)
        gather(h, 3, xm, zl, to_xp)
        to_sibling(h, 2, xm, zl)
        gathered(h, 4, xp, zl, to_xp)
        to_sibling(h, 3, xp, zl)
        gathered(h, 5, xp, zo, to_xp)
        gather(h, 6, xp, zo, to_xm)
        to_sibling(h, 4, xp, zo)
        gathered(h, 2, xm, zo, to_xm)
        to_sibling(h, 5, xm, zo)

    def gather_end(h):
        gathered(h, 3, xo, zl, to_xm)
        to_sibling(h, 6, xo, zl)
        gathered(h, 6, xo, zo, to_xp)
        to_sibling(h, 7, xo, zo)
        for n, (xx, zz) in enumerate(
            ((x, zl), (x, zo), (xm, zl), (xp, zl), (xp, zo), (xm, zo), (xo, zl), (xo, zo))
        ):
            arrived(rblk(h, xx, zz, co), k_s.at[15 * h + 7 + n], k_r.at[15 * h + 7 + n], to_co)

    for h in range(WAVES):
        gather_zl(h)
    gather_own(0)
    gather_own(1)

    def rotate_back():
        p_arrived(1)
        arrived(zrcv, p_s.at[12], p_r.at[12], to_zl)

        @pl.loop(0, 8)
        def _(i):
            rows = pl.ds(pl.multiple_of(i * 16, 16), 16)
            s = (
                pbuf[0, zl, rows, :].astype(F32)
                + rsb[1, 0, rows, :].astype(F32)
                + rsb[1, 1, rows, :].astype(F32)
                + zrcv[rows, :].astype(F32)
            ).astype(BF16)
            hb[2 * i] = s[:, :HALF]
            hb[2 * i + 1] = s[:, HALF:]

        a2a_start(hb, r3, 0)

    def project(h):
        @pl.loop(0, 2)
        def _(par):
            a = rot[par, :, WR * h:WR * h + WR].reshape(8 * WR, WIDTH)
            for n in range(2):
                cols = slice(n * 256, n * 256 + 256)
                p = jnp.dot(a, wq[c, :, cols], preferred_element_type=F32)
                lo[h, par, :, :, cols] = p.astype(BF16).reshape(8, WR, 256)

    def lob(h, yy, par):
        return lo.at[h, par, pl.ds(2 * yy, 2)]

    def tsend(h, n, src, dst, dev):
        send(src, dst, t_s.at[10 * h + n], t_r.at[10 * h + n], dev)

    def tarrived(h, n, dst, dev):
        arrived(dst, t_s.at[10 * h + n], t_r.at[10 * h + n], dev)

    def out_y1(h):
        project(h)
        tsend(h, 0, lob(h, yo, 0), ta.at[h, 0], to_yp)
        tsend(h, 1, lob(h, yo, 1), ta.at[h, 1], to_ym)
        tsend(h, 2, lob(h, yp, 1), tb.at[h, 0, 1], to_yp)
        tsend(h, 3, lob(h, ym, 0), tb.at[h, 1, 0], to_ym)

    def add_to(v, u):
        v[...] = (v[...].astype(F32) + u[...].astype(F32)).astype(BF16)

    def out_y2(h):
        tarrived(h, 0, ta.at[h, 0], to_ym)
        add_to(lob(h, yp, 0), ta.at[h, 0])
        tsend(h, 4, lob(h, yp, 0), tb.at[h, 0, 0], to_yp)
        tarrived(h, 1, ta.at[h, 1], to_yp)
        add_to(lob(h, ym, 1), ta.at[h, 1])
        tsend(h, 5, lob(h, ym, 1), tb.at[h, 1, 1], to_ym)

    def lzh(h, hh, left):
        return lz.at[h, hh % 2, hh // 2, :, pl.ds(0 if left else 256, 256)]

    def out_z1(h):
        tarrived(h, 2, tb.at[h, 0, 1], to_ym)
        tarrived(h, 3, tb.at[h, 1, 0], to_yp)
        tarrived(h, 4, tb.at[h, 0, 0], to_ym)
        tarrived(h, 5, tb.at[h, 1, 1], to_yp)
        for par in range(2):
            lz[h, par] = (
                lob(h, y, par)[...].astype(F32) + tb[h, 0, par].astype(F32) + tb[h, 1, par].astype(F32)
            ).astype(BF16)
        tsend(h, 6, lzh(h, ho, True), tc.at[h, 0], to_hp)
        tsend(h, 7, lzh(h, ho, False), tc.at[h, 1], to_hm)

    def out_z2(h):
        tarrived(h, 6, tc.at[h, 0], to_hm)
        add_to(lzh(h, hp, True), tc.at[h, 0])
        tsend(h, 8, lz.at[h, hp % 2, hp // 2], td.at[h, 0], to_hp)
        tarrived(h, 7, tc.at[h, 1], to_hp)
        add_to(lzh(h, hm, False), tc.at[h, 1])
        tsend(h, 9, lz.at[h, hm % 2, hm // 2], td.at[h, 1], to_hm)

    def out_end(h):
        tarrived(h, 8, td.at[h, 0], to_hm)
        tarrived(h, 9, td.at[h, 1], to_hp)
        lov[WR * h:WR * h + WR, :] = (
            lz[h, zh % 2, zh // 2].astype(F32) + td[h, 0].astype(F32) + td[h, 1].astype(F32)
        ).astype(BF16)

    def down(half, lo_n, hi_n):
        @pl.loop(lo_n, hi_n)
        def _(n):
            cols = pl.ds(pl.multiple_of(n * 256, 256), 256)
            acc = None
            for par in range(2):
                a = rot[par, :, 64 * half:64 * half + 64, cols].reshape(512, 256)
                p = tn(a, gall[c, par, :, 64 * half:64 * half + 64].reshape(512, FEAT))
                acc = p if acc is None else acc + p
            gdv[cols, :] = acc if half == 0 else (gdv[cols, :] + acc) * dsq[cols, :]

    stores = []

    def store(src, dst):
        d = pltpu.make_async_copy(src, dst, o_s.at[len(stores)])
        d.start()
        stores.append(d)

    rotate_back()
    gather_partner(0)
    gather_on(0)
    gather_own(2)
    gather_partner(1)
    gather_end(0)
    out_y1(0)
    gather_on(1)
    gather_own(3)
    gather_partner(2)
    gather_end(1)
    out_y1(1)
    out_y2(0)
    a2a_wait(hb, r3, 0)
    walsh(16, r3, s4)
    a2a_start(s4, r4, 1)
    gather_on(2)
    gather_partner(3)
    gather_end(2)
    out_y1(2)
    out_z1(0)
    out_y2(1)
    gather_on(3)
    down(0, 0, 7)
    out_z2(0)
    out_z1(1)
    out_y2(2)
    gather_end(3)
    out_y1(3)
    out_z2(1)
    out_z1(2)
    down(1, 0, 3)
    out_y2(3)
    out_z2(2)
    down(1, 3, 4)
    store(gdv.at[pl.ds(0, 1024)], gd_out.at[pl.ds(0, 1024)])
    out_z1(3)
    down(1, 4, 7)
    store(gdv.at[pl.ds(1024, 768)], gd_out.at[pl.ds(1024, 768)])
    out_z2(3)
    a2a_wait(s4, r4, 1)

    def block_of(m):
        j, k = m // 7, m % 7
        return jnp.concatenate([r4[2 * i + j, :, 128 * k:128 * k + 128] for i in range(8)], axis=0)

    local_walsh(block_of)

    @pl.loop(0, 8)
    def _(i):
        rows = pl.ds(pl.multiple_of(i * 16, 16), 16)
        for m in range(7):
            evn = uu[0, rows, :] * float(COSINE[m, 0])
            odd = uu[1, rows, :] * float(COSINE[m, 1])
            for n in range(2, COS, 2):
                evn = evn + uu[n, rows, :] * float(COSINE[m, n])
                odd = odd + uu[n + 1, rows, :] * float(COSINE[m, n + 1])
            for mm, val in ((m, evn + odd), (13 - m, evn - odd)):
                cols = slice(128 * mm, 128 * mm + 128)
                gh = val * sign[:, cols]
                v = gate[rows, cols].astype(F32)
                sigma = jax.nn.sigmoid(v)
                ggv[rows, cols] = (
                    gh * up[rows, cols].astype(F32) * sigma * (1.0 + v * (1.0 - sigma))
                ).astype(BF16)
                guv[rows, cols] = (gh * (v * sigma)).astype(BF16)

    store(ggv, gg_out)
    store(guv, gu_out)
    for h in range(WAVES):
        out_end(h)
    store(lov, lo_out)
    for d in sent:
        d.wait_send()
    for d in stores:
        d.wait()


def finish(lo_i, gd_i, gg_i, gu_i, lo_o, gd_o, gg_o, gu_o, lo_v, gd_v, gg_v, gu_v, sem_i, sem_o):
    pieces = []
    for n in range(7):
        rows = pl.ds(256 * n, 256)
        pieces.append((gd_i.at[rows], gd_v.at[rows], gd_o.at[rows]))
    pieces += [(gg_i, gg_v, gg_o), (gu_i, gu_v, gu_o), (lo_i, lo_v, lo_o)]
    loads = [pltpu.make_async_copy(a, b, sem_i.at[n]) for n, (a, b, _) in enumerate(pieces)]
    stores = [pltpu.make_async_copy(b, o, sem_o.at[n]) for n, (_, b, o) in enumerate(pieces)]
    for d in loads:
        d.start()
    for d, e in zip(loads, stores):
        d.wait()
        e.start()
    for e in stores:
        e.wait()


def on_device(gate_pre, up_pre, down_rotated, exponents, signs, out_grad):
    anywhere = pl.BlockSpec(memory_space=pl.ANY)
    blocks = pltpu.VMEM((16, 16, HALF), BF16)
    dma = pltpu.SemaphoreType.DMA
    out_shape = (
        jax.ShapeDtypeStruct((ROWS, FEAT), BF16),
        jax.ShapeDtypeStruct((WIDTH, FEAT), F32),
        jax.ShapeDtypeStruct((ROWS, WIDTH), BF16),
        jax.ShapeDtypeStruct((ROWS, WIDTH), BF16),
    )
    outs = pl.pallas_call(
        kernel,
        out_shape=out_shape,
        in_specs=[anywhere] * 7,
        out_specs=(anywhere,) * 4,
        scratch_shapes=[
            pltpu.VMEM((ROWS, WIDTH), BF16),
            pltpu.VMEM((ROWS, WIDTH), BF16),
            pltpu.VMEM((WIDTH, FEAT), BF16),
            pltpu.VMEM((COS, FEAT), jnp.int32),
            pltpu.VMEM((WIDTH,), jnp.int32),
            pltpu.VMEM((WALSH, WALSH), BF16),
        ]
        + [pltpu.VMEM((4, 32, WIDTH), BF16)] * 7
        + [blocks] * 4
        + [
            pltpu.VMEM((COS, ROWS, WALSH), F32),
            pltpu.VMEM((2, 2, 8, ROWS, FEAT), BF16),
            pltpu.VMEM((2, WIDTH, FEAT), BF16),
            pltpu.VMEM((WIDTH, FEAT), F32),
            pltpu.VMEM((2, 8, ROWS, WIDTH), BF16),
            pltpu.VMEM((4, 2, ROWS, WIDTH), BF16),
            pltpu.VMEM((2, 2, 64, WIDTH), BF16),
            pltpu.VMEM((2, 2, ROWS, WIDTH), BF16),
            pltpu.VMEM((ROWS, WIDTH), BF16),
            pltpu.VMEM((ROWS, WIDTH), BF16),
            pltpu.VMEM((WAVES, 2, 8, WR, FEAT), BF16),
            pltpu.VMEM((WAVES, 2, 2, WR, FEAT), BF16),
            pltpu.VMEM((WAVES, 2, 2, 2, WR, FEAT), BF16),
            pltpu.VMEM((WAVES, 2, 2, WR, FEAT), BF16),
            pltpu.VMEM((WAVES, 2, WR, 256), BF16),
            pltpu.VMEM((WAVES, 2, WR, FEAT), BF16),
            pltpu.VMEM((ROWS, FEAT), BF16),
            pltpu.VMEM((WIDTH, FEAT), F32),
            pltpu.VMEM((ROWS, WIDTH), BF16),
            pltpu.VMEM((ROWS, WIDTH), BF16),
            dma((7,)), dma((5,)),
            dma((4, 4)), dma((4, 4)),
            dma((2, 16)), dma((2, 16)),
            dma((30,)), dma((30,)),
            dma((5,)), dma((5,)),
            dma((13,)), dma((13,)),
            dma((15 * WAVES,)), dma((15 * WAVES,)),
            dma((10 * WAVES,)), dma((10 * WAVES,)),
        ],
        compiler_params=pltpu.CompilerParams(
            collective_id=0, has_side_effects=True, vmem_limit_bytes=60 * 1024 * 1024
        ),
        cost_estimate=pl.CostEstimate(
            flops=11_300_000_000, bytes_accessed=9_000_000, transcendentals=2_000_000
        ),
    )(
        gate_pre, up_pre, down_rotated, exponents, signs, out_grad,
        jnp.asarray(walsh_signs(WALSH)),
    )
    return pl.pallas_call(
        finish,
        out_shape=out_shape,
        in_specs=[anywhere] * 4,
        out_specs=(anywhere,) * 4,
        scratch_shapes=[pltpu.VMEM(o.shape, o.dtype) for o in out_shape] + [dma((10,)), dma((10,))],
        compiler_params=pltpu.CompilerParams(vmem_limit_bytes=60 * 1024 * 1024),
    )(*outs)


def solution(mesh):
    return jax.shard_map(
        on_device,
        mesh=mesh,
        in_specs=(
            P("dp", "tensor"),
            P("dp", "tensor"),
            P("tensor", "dp"),
            P("tensor", "dp"),
            P("tensor"),
            P("tensor", "dp"),
        ),
        out_specs=(P("tensor", "dp"), P("tensor", "dp"), P("dp", "tensor"), P("dp", "tensor")),
        check_vma=False,
    )
```

time: 501 us -> 134 us (0.27)
  waiting for transfers between devices: 406 us -> 0 us
  Pallas kernels: 0 us -> 132 us
  matrix products: 32.4 us -> 0 us
  starting transfers between devices: 22.5 us -> 0 us
  local copies, waits for them, and re-layouts: 14.7 us -> 0 us
  between operations: 14 us -> 0.64 us
  other arithmetic: 10.7 us -> 0 us
    all_gather x2 -> x0, waiting for transfers between devices: 136 us -> none  [the longest x1 76.3 us: on_device(): all_rows = lax.all_gather(rotated, 'dp', axis=0, tiled=True)]
    pallas_call x0 -> x2, Pallas kernels: none -> 132 us  [the longest x1 128 us: on_device(): pl.pallas_call(kernel, out_shape=out_shape, in_specs=[anywhere] * 7, out_...]
    ppermute x8 -> x0, waiting for transfers between devices: 111 us -> none  [partner_2(): lax.ppermute(array, axis, [(i, i ^ 1 << distance) for i in range(lax.axis...]
    unnamed x5 -> x0, waiting for transfers between devices: 86.7 us -> none
    reduce_scatter x1 -> x0, waiting for transfers between devices: 72.7 us -> none  [on_device(): lax.psum_scatter(jnp.dot(piece, weight_q, preferred_element_type=jnp.floa...]
    dot_general x7 -> x0, matrix products: 32.4 us -> none  [the longest x1 10.7 us: on_device(): lax.dot_general(all_rows, grad_all, (((0,), (0,)), ((), ())), preferred_e...]
    ppermute x8 -> x0, starting transfers between devices: 22.1 us -> none  [partner_2(): lax.ppermute(array, axis, [(i, i ^ 1 << distance) for i in range(lax.axis...]
    unnamed x24 -> x0, local copies, waits for them, and re-layouts: 13.8 us -> none
  transfers between devices with their start and end apart: 12 -> 0, of which waited for: 12 -> 0; matrix products, arithmetic and copies ran while one was open for 4% -> 0% of each run, Pallas kernels for 0% -> 0%
where the time goes in v2:
time: 134 us; the launch traced here: 133 us
  Pallas kernels  132 us (99%)
    pallas_call x1, Pallas kernels, on_device(): pl.pallas_call(kernel, out_shape=out_shape, in_specs=[anywhere] * 7, out_...  128 us
    pallas_call x1, Pallas kernels, on_device(): pl.pallas_call(finish, out_shape=out_shape, in_specs=[anywhere] * 4, out_...  4.05 us

profile of v2, /device:TPU:2, one launch (start us, length us, event | category | flops | bytes accessed | tf_op | source)
XLA Modules:
  0.0 132.6 jit_solution(1198757527817269139)
XLA Ops:
  0.6 127.9 %shard_map.102 = (bf16[128,512]{1,0:T(8,128)(2,1)}, f32[1792,512]{1,0:T(8,128)}, bf16[128,1792]{1,0:T(8,128)(2,1)}, bf16[128,1792]{1,0:T(8,128)(2,1)}) custom-call(bf16[128,1792]{1,0:T(8,128)(2,1)} %gate_h.1, bf16[128,1792]{1,0:T(8,128)(2,1)} %up_h.1, bf16[1792,512]{1,0:T(8,128)(2,1)} %w_h.1, s32[14,512]{1,0:T(8,128)} %ex_h.1, s32[1792]{0:T(1024)} %sg_h.1, ...), custom_call_target="tpu_custom_call" | custom-call | flops 11299999744 | bytes 9000000 | tf_op jit(solution)/shard_map/pallas_call | solution.py:643
  128.5 4.0 %shard_map.103 = (bf16[128,512]{1,0:T(8,128)(2,1)}, f32[1792,512]{1,0:T(8,128)}, bf16[128,1792]{1,0:T(8,128)(2,1)}, bf16[128,1792]{1,0:T(8,128)(2,1)}) custom-call(bf16[128,512]{1,0:T(8,128)(2,1)} %get-tuple-element.8.lo_i, f32[1792,512]{1,0:T(8,128)} %get-tuple-element.9.gd_i, bf16[128,1792]{1,0:T(8,128)(2,1)} %get-tuple-element.10.gg_i, ...), custom_call_target="tpu_custom_call" | custom-call | tf_op jit(solution)/shard_map/pallas_call | solution.py:698

commit v3 on v2

--- a/solution.py
+++ b/solution.py
@@ -74,7 +74,7 @@
     f0, f1, f2, f3, f4, f5, f6, hb, r3, s4, r4, uu,
     gall, wq, dsq, rot,
     pbuf, rsa, rsb, zsnd, zrcv,
-    lo, ta, tb, lz, tc, td,
+    lo, tb, lz, td,
     lov, gdv, ggv, guv,
     i_s, o_s, f_s, f_r, a_s, a_r, g_s, g_r, c_s, c_r, p_s, p_r, k_s, k_r, t_s, t_r,
 ):
@@ -428,8 +428,10 @@
         ):
             arrived(rblk(h, xx, zz, co), k_s.at[15 * h + 7 + n], k_r.at[15 * h + 7 + n], to_co)
 
-    for h in range(WAVES):
-        gather_zl(h)
+    gather_zl(0)
+    gather_zl(1)
+    gather_zl(2)
+    gather_zl(3)
     gather_own(0)
     gather_own(1)
 
@@ -458,64 +460,36 @@
             for n in range(2):
                 cols = slice(n * 256, n * 256 + 256)
                 p = jnp.dot(a, wq[c, :, cols], preferred_element_type=F32)
-                lo[h, par, :, :, cols] = p.astype(BF16).reshape(8, WR, 256)
-
-    def lob(h, yy, par):
-        return lo.at[h, par, pl.ds(2 * yy, 2)]
-
-    def tsend(h, n, src, dst, dev):
-        send(src, dst, t_s.at[10 * h + n], t_r.at[10 * h + n], dev)
-
-    def tarrived(h, n, dst, dev):
-        arrived(dst, t_s.at[10 * h + n], t_r.at[10 * h + n], dev)
-
-    def out_y1(h):
+                lo[h, :, par, :, :, cols] = p.astype(BF16).reshape(4, 2, WR, 256)
+
+    def out_y(h):
         project(h)
-        tsend(h, 0, lob(h, yo, 0), ta.at[h, 0], to_yp)
-        tsend(h, 1, lob(h, yo, 1), ta.at[h, 1], to_ym)
-        tsend(h, 2, lob(h, yp, 1), tb.at[h, 0, 1], to_yp)
-        tsend(h, 3, lob(h, ym, 0), tb.at[h, 1, 0], to_ym)
-
-    def add_to(v, u):
-        v[...] = (v[...].astype(F32) + u[...].astype(F32)).astype(BF16)
-
-    def out_y2(h):
-        tarrived(h, 0, ta.at[h, 0], to_ym)
-        add_to(lob(h, yp, 0), ta.at[h, 0])
-        tsend(h, 4, lob(h, yp, 0), tb.at[h, 0, 0], to_yp)
-        tarrived(h, 1, ta.at[h, 1], to_yp)
-        add_to(lob(h, ym, 1), ta.at[h, 1])
-        tsend(h, 5, lob(h, ym, 1), tb.at[h, 1, 1], to_ym)
-
-    def lzh(h, hh, left):
-        return lz.at[h, hh % 2, hh // 2, :, pl.ds(0 if left else 256, 256)]
-
-    def out_z1(h):
-        tarrived(h, 2, tb.at[h, 0, 1], to_ym)
-        tarrived(h, 3, tb.at[h, 1, 0], to_yp)
-        tarrived(h, 4, tb.at[h, 0, 0], to_ym)
-        tarrived(h, 5, tb.at[h, 1, 1], to_yp)
+        for j in range(1, 4):
+            n = 6 * h + j - 1
+            d = (y + j) % 4
+            send(lo.at[h, d], tb.at[h, j - 1], t_s.at[n], t_r.at[n], (dp, d * 4 + zh))
+
+    def out_z(h):
+        for j in range(1, 4):
+            n = 6 * h + j - 1
+            arrived(tb.at[h, j - 1], t_s.at[n], t_r.at[n], (dp, (y + 4 - j) % 4 * 4 + zh))
         for par in range(2):
-            lz[h, par] = (
-                lob(h, y, par)[...].astype(F32) + tb[h, 0, par].astype(F32) + tb[h, 1, par].astype(F32)
-            ).astype(BF16)
-        tsend(h, 6, lzh(h, ho, True), tc.at[h, 0], to_hp)
-        tsend(h, 7, lzh(h, ho, False), tc.at[h, 1], to_hm)
-
-    def out_z2(h):
-        tarrived(h, 6, tc.at[h, 0], to_hm)
-        add_to(lzh(h, hp, True), tc.at[h, 0])
-        tsend(h, 8, lz.at[h, hp % 2, hp // 2], td.at[h, 0], to_hp)
-        tarrived(h, 7, tc.at[h, 1], to_hp)
-        add_to(lzh(h, hm, False), tc.at[h, 1])
-        tsend(h, 9, lz.at[h, hm % 2, hm // 2], td.at[h, 1], to_hm)
+            total = lo[h, y, par].astype(F32)
+            for j in range(3):
+                total = total + tb[h, j, par].astype(F32)
+            lz[h, par] = total.astype(BF16)
+        for j in range(1, 4):
+            n = 6 * h + j + 2
+            d = (zh + j) % 4
+            send(lz.at[h, d % 2, d // 2], td.at[h, j - 1], t_s.at[n], t_r.at[n], (dp, y * 4 + d))
 
     def out_end(h):
-        tarrived(h, 8, td.at[h, 0], to_hm)
-        tarrived(h, 9, td.at[h, 1], to_hp)
-        lov[WR * h:WR * h + WR, :] = (
-            lz[h, zh % 2, zh // 2].astype(F32) + td[h, 0].astype(F32) + td[h, 1].astype(F32)
-        ).astype(BF16)
+        total = lz[h, zh % 2, zh // 2].astype(F32)
+        for j in range(1, 4):
+            n = 6 * h + j + 2
+            arrived(td.at[h, j - 1], t_s.at[n], t_r.at[n], (dp, y * 4 + (zh + 4 - j) % 4))
+            total = total + td[h, j - 1].astype(F32)
+        lov[WR * h:WR * h + WR, :] = total.astype(BF16)
 
     def down(half, lo_n, hi_n):
         @pl.loop(lo_n, hi_n)
@@ -541,40 +515,32 @@
     gather_own(2)
     gather_partner(1)
     gather_end(0)
-    out_y1(0)
+    out_y(0)
     gather_on(1)
     gather_own(3)
     gather_partner(2)
-    gather_end(1)
-    out_y1(1)
-    out_y2(0)
     a2a_wait(hb, r3, 0)
     walsh(16, r3, s4)
     a2a_start(s4, r4, 1)
+    gather_end(1)
+    out_y(1)
     gather_on(2)
     gather_partner(3)
     gather_end(2)
-    out_y1(2)
-    out_z1(0)
-    out_y2(1)
+    out_y(2)
+    out_z(0)
     gather_on(3)
-    down(0, 0, 7)
-    out_z2(0)
-    out_z1(1)
-    out_y2(2)
+    out_z(1)
+    down(0, 0, 4)
     gather_end(3)
-    out_y1(3)
-    out_z2(1)
-    out_z1(2)
-    down(1, 0, 3)
-    out_y2(3)
-    out_z2(2)
-    down(1, 3, 4)
+    out_y(3)
+    out_z(2)
+    down(0, 4, 7)
+    down(1, 0, 4)
     store(gdv.at[pl.ds(0, 1024)], gd_out.at[pl.ds(0, 1024)])
-    out_z1(3)
+    out_z(3)
     down(1, 4, 7)
     store(gdv.at[pl.ds(1024, 768)], gd_out.at[pl.ds(1024, 768)])
-    out_z2(3)
     a2a_wait(s4, r4, 1)
 
     def block_of(m):
@@ -666,12 +632,10 @@
             pltpu.VMEM((2, 2, ROWS, WIDTH), BF16),
             pltpu.VMEM((ROWS, WIDTH), BF16),
             pltpu.VMEM((ROWS, WIDTH), BF16),
-            pltpu.VMEM((WAVES, 2, 8, WR, FEAT), BF16),
+            pltpu.VMEM((WAVES, 4, 2, 2, WR, FEAT), BF16),
+            pltpu.VMEM((WAVES, 3, 2, 2, WR, FEAT), BF16),
             pltpu.VMEM((WAVES, 2, 2, WR, FEAT), BF16),
-            pltpu.VMEM((WAVES, 2, 2, 2, WR, FEAT), BF16),
-            pltpu.VMEM((WAVES, 2, 2, WR, FEAT), BF16),
-            pltpu.VMEM((WAVES, 2, WR, 256), BF16),
-            pltpu.VMEM((WAVES, 2, WR, FEAT), BF16),
+            pltpu.VMEM((WAVES, 3, WR, FEAT), BF16),
             pltpu.VMEM((ROWS, FEAT), BF16),
             pltpu.VMEM((WIDTH, FEAT), F32),
             pltpu.VMEM((ROWS, WIDTH), BF16),
@@ -683,7 +647,7 @@
             dma((5,)), dma((5,)),
             dma((13,)), dma((13,)),
             dma((15 * WAVES,)), dma((15 * WAVES,)),
-            dma((10 * WAVES,)), dma((10 * WAVES,)),
+            dma((6 * WAVES,)), dma((6 * WAVES,)),
         ],
         compiler_params=pltpu.CompilerParams(
             collective_id=0, has_side_effects=True, vmem_limit_bytes=60 * 1024 * 1024

time: 134 us -> 129 us (0.963)
  Pallas kernels: 132 us -> 128 us
    pallas_call x1, Pallas kernels: 128 us -> 124 us  [on_device(): pl.pallas_call(kernel, out_shape=out_shape, in_specs=[anywhere] * 7, out_...]
where the time goes in v3:
time: 129 us; the launch traced here: 128 us
  Pallas kernels  128 us (99%)
    pallas_call x1, Pallas kernels, on_device(): pl.pallas_call(kernel, out_shape=out_shape, in_specs=[anywhere] * 7, out_...  124 us
    pallas_call x1, Pallas kernels, on_device(): pl.pallas_call(finish, out_shape=out_shape, in_specs=[anywhere] * 4, out_...  4.05 us

profile of v3, /device:TPU:2, one launch (start us, length us, event | category | flops | bytes accessed | tf_op | source)
XLA Modules:
  0.0 128.5 jit_solution(9956649259198386673)
XLA Ops:
  0.6 123.8 %shard_map.102 = (bf16[128,512]{1,0:T(8,128)(2,1)}, f32[1792,512]{1,0:T(8,128)}, bf16[128,1792]{1,0:T(8,128)(2,1)}, bf16[128,1792]{1,0:T(8,128)(2,1)}) custom-call(bf16[128,1792]{1,0:T(8,128)(2,1)} %gate_h.1, bf16[128,1792]{1,0:T(8,128)(2,1)} %up_h.1, bf16[1792,512]{1,0:T(8,128)(2,1)} %w_h.1, s32[14,512]{1,0:T(8,128)} %ex_h.1, s32[1792]{0:T(1024)} %sg_h.1, ...), custom_call_target="tpu_custom_call" | custom-call | flops 11299999744 | bytes 9000000 | tf_op jit(solution)/shard_map/pallas_call | solution.py:609
  124.4 4.0 %shard_map.103 = (bf16[128,512]{1,0:T(8,128)(2,1)}, f32[1792,512]{1,0:T(8,128)}, bf16[128,1792]{1,0:T(8,128)(2,1)}, bf16[128,1792]{1,0:T(8,128)(2,1)}) custom-call(bf16[128,512]{1,0:T(8,128)(2,1)} %get-tuple-element.8.lo_i, f32[1792,512]{1,0:T(8,128)} %get-tuple-element.9.gd_i, bf16[128,1792]{1,0:T(8,128)(2,1)} %get-tuple-element.10.gg_i, ...), custom_call_target="tpu_custom_call" | custom-call | tf_op jit(solution)/shard_map/pallas_call | solution.py:662

commit v4 on v3

--- a/solution.py
+++ b/solution.py
@@ -334,11 +334,11 @@
     stage_wait(f0, f1, 0)
     walsh(4, f1, f2)
     stage_start(f2, f3, 1)
+    stage_wait(f2, f3, 1)
+    stage_start(f3, f4, 2)
     p_onward(0, zo)
     for d in (p_far[2], p_far[3], p_next[1], p_last[1]):
         d.start()
-    stage_wait(f2, f3, 1)
-    stage_start(f3, f4, 2)
 
     p_arrived(0)
 

time: 129 us -> 132 us (1.023)
  Pallas kernels: 128 us -> 131 us
    pallas_call x1, Pallas kernels: 124 us -> 127 us  [on_device(): pl.pallas_call(kernel, out_shape=out_shape, in_specs=[anywhere] * 7, out_...]
where the time goes in v4:
time: 132 us
  Pallas kernels  131 us (99%)
    pallas_call x1, Pallas kernels, on_device(): pl.pallas_call(kernel, out_shape=out_shape, in_specs=[anywhere] * 7, out_...  127 us
    pallas_call x1, Pallas kernels, on_device(): pl.pallas_call(finish, out_shape=out_shape, in_specs=[anywhere] * 4, out_...  4.05 us

profile of v4, /device:TPU:2, one launch (start us, length us, event | category | flops | bytes accessed | tf_op | source)
XLA Modules:
  0.0 131.7 jit_solution(13131873741976253352)
XLA Ops:
  0.6 127.0 %shard_map.102 = (bf16[128,512]{1,0:T(8,128)(2,1)}, f32[1792,512]{1,0:T(8,128)}, bf16[128,1792]{1,0:T(8,128)(2,1)}, bf16[128,1792]{1,0:T(8,128)(2,1)}) custom-call(bf16[128,1792]{1,0:T(8,128)(2,1)} %gate_h.1, bf16[128,1792]{1,0:T(8,128)(2,1)} %up_h.1, bf16[1792,512]{1,0:T(8,128)(2,1)} %w_h.1, s32[14,512]{1,0:T(8,128)} %ex_h.1, s32[1792]{0:T(1024)} %sg_h.1, ...), custom_call_target="tpu_custom_call" | custom-call | flops 11299999744 | bytes 9000000 | tf_op jit(solution)/shard_map/pallas_call | solution.py:609
  127.6 4.0 %shard_map.103 = (bf16[128,512]{1,0:T(8,128)(2,1)}, f32[1792,512]{1,0:T(8,128)}, bf16[128,1792]{1,0:T(8,128)(2,1)}, bf16[128,1792]{1,0:T(8,128)(2,1)}) custom-call(bf16[128,512]{1,0:T(8,128)(2,1)} %get-tuple-element.8.lo_i, f32[1792,512]{1,0:T(8,128)} %get-tuple-element.9.gd_i, bf16[128,1792]{1,0:T(8,128)(2,1)} %get-tuple-element.10.gg_i, ...), custom_call_target="tpu_custom_call" | custom-call | tf_op jit(solution)/shard_map/pallas_call | solution.py:662
